TPU v7x, 32 devices: a whole 2x2x4 slice. The times are simulated.
32 devices in a mesh: groups: 2 (over x), ctx: 16 (over z, y, core).
Axes of the slice: x: 2, y: 2, z: 4, core: 2. Of those that a mesh axis runs over, the one named last changes fastest.
Arguments:
- context: bfloat16 [96, 256, 1024], P(('groups', 'ctx')), parts along dimension 0, may hold values from -6 to 6
- counts: int32 [32], P('groups'), parts along dimension 0, may hold values from 1 to 3, as said below
- queries: bfloat16 [128, 4096], P(('groups', 'ctx')), parts along dimension 0, may hold values from -120 to 120
- norm_gain: bfloat16 [1024], replicated, may hold values from 0.099609375 to 1.8984375
- w_query: bfloat16 [1024, 1024], replicated, may hold values from -1 to 1
- w_key: bfloat16 [1024, 1024], replicated, may hold values from -9 to 9
- w_value: bfloat16 [1024, 1024], replicated, may hold values from -0.1875 to 0.1875
- w_out: bfloat16 [1024, 1024], replicated, may hold values from -0.1875 to 0.1875
- final_gain: bfloat16 [1024], replicated, may hold values from 0.099609375 to 1.8984375
- w_kv: bfloat16 [1024, 2048], P(None, 'ctx'), may hold values from -0.1875 to 0.1875
Outputs:
- attended_context: bfloat16 [128, 4096], P(('groups', 'ctx')), parts along dimension 0
There are 2 independent parts, one for each index of `groups`. A program takes and returns all parts, laid end to end along the dimension named above; an argument that names none is the same for every part. Nothing has to cross between parts.
Inputs may be any that keep to these rules, and one draw needn't show every extreme that they name: Device d's slots are d * 3 to d * 3 + 2, and only the first counts[d] of them hold live blocks. The largest count equals 3 in every draw. For every d below 8, counts[d] + counts[d + 8] is at most 4, and equals it for some d in every draw.
All inputs are finite; a program needn't handle non-finite values.
Results may differ from a plain program's by a relative error of at most 0.025.
The roundings to bfloat16 on the way count: a program that leaves them out, or rounds other values in their place, can miss the bound.
Values may be sent and summed in bfloat16 or wider, within the bound.
No kernel may reach another device: no remote copies, remote signals or barrier semaphores. Data moves between devices by JAX's collectives and lax.ppermute only.
A program may use at most 128 MiB of HBM per device.

v0:
```python
import functools
import math

import jax
import jax.numpy as jnp
import numpy as np
from jax import lax
from jax.experimental import pallas as pl
from jax.experimental.pallas import tpu as pltpu
from jax.sharding import PartitionSpec as P

D_ENC = 1024
ENC_HEADS = 16
ENC_HD = 64
BLOCK = 256
KV_HEADS = 8
HEAD_DIM = 128
Q_HEADS = 32
GROUP = 4
QW = 4096
CAP = 3
HALF_HEADS = KV_HEADS // 2
LANES = 128
CHIPS = 8
ROWS = 4
LINES = ROWS * GROUP
F32 = jnp.float32
BF16 = jnp.bfloat16
VMEM = pl.BlockSpec(memory_space=pltpu.VMEM)
SMEM = pl.BlockSpec(memory_space=pltpu.SMEM)
HBM = pl.BlockSpec(memory_space=pltpu.HBM)
PARTS = 4
PART = D_ENC // PARTS


def root_scale(values, gain):
    values = values.astype(F32)
    return (
        values
        * lax.rsqrt(jnp.mean(values * values, axis=-1, keepdims=True) + 1e-05)
        * gain.astype(F32)
    )


def rotary_lanes():
    position = np.arange(BLOCK, dtype=np.float64)[:, None]
    frequency = 10000.0 ** (-2.0 * np.arange(ENC_HD // 2) / ENC_HD)
    angle = position * frequency[None, :]
    cosine, sine = np.cos(angle), np.sin(angle)
    return (
        jnp.asarray(np.concatenate([cosine, cosine, cosine, cosine], axis=1), F32),
        jnp.asarray(np.concatenate([-sine, sine, -sine, sine], axis=1), F32),
    )


def live_counts(counts_ref):
    me = lax.axis_index("ctx")
    own, other = counts_ref[me], counts_ref[me + 1 - 2 * lax.rem(me, 2)]
    gives = jnp.where((own == 3) & (other == 1), 1, 0)
    takes = jnp.where((own == 1) & (other == 3), 1, 0)
    return own - gives + takes, other + gives - takes, takes


def query_kernel(query_ref, keep_ref, give_ref):
    core = lax.rem(lax.axis_index("ctx"), 2)
    width = GROUP * HEAD_DIM
    for out_ref, parity in ((keep_ref, core), (give_ref, 1 - core)):
        for head in range(HALF_HEADS):
            start = pl.multiple_of((2 * head + parity) * width, width)
            rows = query_ref[:, pl.ds(start, width)].astype(F32)
            out_ref[head] = jnp.concatenate(
                [rows[:, g * LANES : (g + 1) * LANES] for g in range(GROUP)], axis=0
            ).astype(BF16)


def split_queries(queries):
    shape = jax.ShapeDtypeStruct((HALF_HEADS, LINES, LANES), BF16)
    return pl.pallas_call(
        query_kernel, out_shape=(shape, shape), in_specs=[VMEM], out_specs=(VMEM, VMEM),
    )(queries)


def encoder_kernel(slot, counts_ref, context_ref, taken_ref, wq_ref, wk_ref, wv_ref, wo_ref, gain_ref, fgain_ref,
                   cos_ref, sin_ref, out_ref, mixed_ref, x_ref, q_buf, k_buf, v_buf, o_buf, sems, x_sem):
    live, _, takes = live_counts(counts_ref)

    @pl.when(live > slot)
    def _():
        if slot == 1:
            @pl.when(takes != 0)
            def _():
                pltpu.make_async_copy(taken_ref, x_ref, x_sem).start()

            @pl.when(takes == 0)
            def _():
                pltpu.make_async_copy(context_ref.at[slot], x_ref, x_sem).start()
        else:
            pltpu.make_async_copy(context_ref.at[slot], x_ref, x_sem).start()

        copies = []
        for part in range(PARTS):
            columns = slice(part * PART, (part + 1) * PART)
            copies.append([
                pltpu.make_async_copy(hbm.at[:, columns], buf.at[:, columns], sems.at[part, at])
                for at, (hbm, buf) in enumerate(((wq_ref, q_buf), (wk_ref, k_buf), (wv_ref, v_buf)))
            ])
        for group in copies:
            for copy in group:
                copy.start()
        out_copy = pltpu.make_async_copy(wo_ref, o_buf, sems.at[0, 3])
        out_copy.start()
        pltpu.make_async_copy(context_ref.at[slot], x_ref, x_sem).wait()

        normed = root_scale(x_ref[...], gain_ref[...]).astype(BF16)
        cosine, sine = cos_ref[...], sin_ref[...]
        cosine_query, sine_query = cosine * 0.125, sine * 0.125
        lane = lax.broadcasted_iota(jnp.int32, (BLOCK, LANES), 1)
        lower = (lane % ENC_HD) < ENC_HD // 2
        first = lane < ENC_HD

        def rotate(values, cosine, sine):
            swapped = jnp.where(
                lower,
                pltpu.roll(values, LANES - ENC_HD // 2, 1),
                pltpu.roll(values, ENC_HD // 2, 1),
            )
            return (values * cosine + swapped * sine).astype(BF16)

        for part in range(PARTS):
            columns = slice(part * PART, (part + 1) * PART)
            for copy in copies[part]:
                copy.wait()
            query = jnp.dot(normed, q_buf[:, columns], preferred_element_type=F32)
            key = jnp.dot(normed, k_buf[:, columns], preferred_element_type=F32)
            value = jnp.dot(normed, v_buf[:, columns], preferred_element_type=F32).astype(BF16)
            for pair in range(PART // LANES):
                cut = slice(pair * LANES, (pair + 1) * LANES)
                query_pair = rotate(query[:, cut], cosine_query, sine_query)
                key_pair = rotate(key[:, cut], cosine, sine)
                value_pair = value[:, cut]
                mixed = []
                for head in range(2):
                    own = first if head == 0 else jnp.logical_not(first)
                    scores = lax.dot_general(
                        jnp.where(own, query_pair, jnp.zeros_like(query_pair)), key_pair,
                        (((1,), (1,)), ((), ())), preferred_element_type=F32,
                    )
                    weights = jnp.exp(scores - jnp.max(scores, axis=-1, keepdims=True))
                    weights = weights * (1.0 / jnp.sum(weights, axis=-1, keepdims=True))
                    mixed.append(jnp.dot(weights.astype(BF16), value_pair, preferred_element_type=F32))
                start = part * PART + pair * LANES
                mixed_ref[:, start : start + LANES] = jnp.where(first, mixed[0], mixed[1]).astype(BF16)
        out_copy.wait()
        residual = x_ref[...].astype(F32) + jnp.dot(mixed_ref[...], o_buf[...], preferred_element_type=F32)
        out_ref[...] = root_scale(residual, fgain_ref[...]).astype(BF16)


def encode(slot, counts, context, taken, weights):
    square = pltpu.VMEM((D_ENC, D_ENC), BF16)
    return pl.pallas_call(
        functools.partial(encoder_kernel, slot),
        out_shape=jax.ShapeDtypeStruct((BLOCK, D_ENC), BF16),
        in_specs=[SMEM] + [HBM] * 6 + [VMEM] * 4,
        out_specs=VMEM,
        scratch_shapes=[
            pltpu.VMEM((BLOCK, D_ENC), BF16), pltpu.VMEM((BLOCK, D_ENC), BF16),
            square, square, square, square,
            pltpu.SemaphoreType.DMA((PARTS, 4)), pltpu.SemaphoreType.DMA,
        ],
        compiler_params=pltpu.CompilerParams(vmem_limit_bytes=63 * 2**20),
        cost_estimate=pl.CostEstimate(flops=6 * 10**9, bytes_accessed=9 * 2**20, transcendentals=2**20),
    )(counts, context, taken, *weights)


def three_parts(values):
    high = values.astype(BF16).astype(F32)
    middle = (values - high).astype(BF16).astype(F32)
    return high, middle, values - high - middle


def ring_chips(me):
    z, y = me // 4, lax.rem(me // 2, 2)
    place = jnp.where(z == 3, 2, jnp.where(z == 2, 3, z))
    chips = []
    for step in range(4):
        at = lax.rem(place + 4 - step, 4)
        z = jnp.where(at == 2, 3, jnp.where(at == 3, 2, at))
        chips.append((2 * z + y, 2 * z + 1 - y))
    return chips


def cross_kernel(counts_ref, *refs):
    tokens, loads, rows = refs[:6], refs[6:14], refs[14:18]
    out_ref, token_buf, weight_buf, query_buf, total_ref, top_ref, sum_ref, sems, token_sems, row_sems = refs[18:]
    me = lax.axis_index("ctx")
    core = lax.rem(me, 2)
    own_live, other_live, _ = live_counts(counts_ref)
    chips = ring_chips(me)
    copies = []
    for step in range(4):
        for side in range(2):
            start = pl.multiple_of(chips[step][side] * LANES, LANES)
            copies.append(pltpu.make_async_copy(
                loads[2 * step + side], weight_buf.at[:, pl.ds(start, LANES)], sems.at[2 * step + side]))
    for step in range(4):
        for side in range(2):
            for at, part in ((0, core), (1, 1 - core)):
                start = pl.multiple_of((2 * chips[step][side] + part) * LINES, LINES)
                copies.append(pltpu.make_async_copy(
                    rows[step].at[side, at], query_buf.at[:, pl.ds(start, LINES), :],
                    row_sems.at[4 * step + 2 * side + at]))

    def token_copy(at):
        return pltpu.make_async_copy(tokens[at], token_buf.at[at], token_sems.at[at])

    def live(at):
        return (own_live > at) if at < CAP else (other_live > at - CAP)

    for copy in copies:
        copy.start()
    for at in range(2 * CAP):
        @pl.when(live(at))
        def _():
            token_copy(at).start()
    total_ref[...] = jnp.zeros_like(total_ref)
    sum_ref[...] = jnp.zeros_like(sum_ref)
    top_ref[...] = jnp.full_like(top_ref, -jnp.inf)
    for copy in copies:
        copy.wait()

    for at in range(2 * CAP):
        @pl.when(live(at))
        def _():
            token_copy(at).wait()
            both = jnp.dot(token_buf[at], weight_buf[...], preferred_element_type=F32).astype(BF16)
            for head in range(HALF_HEADS):
                key = both[:, head * LANES : (head + 1) * LANES]
                value = both[:, (HALF_HEADS + head) * LANES : (HALF_HEADS + head + 1) * LANES]
                scores = lax.dot_general(
                    query_buf[head], key, (((1,), (1,)), ((), ())), preferred_element_type=F32
                ) * (1.0 / math.sqrt(HEAD_DIM))
                old_top = top_ref[head]
                new_top = jnp.maximum(old_top, jnp.max(scores, axis=-1, keepdims=True))
                weights = jnp.exp(scores - new_top[:, :1])
                shrink = jnp.exp(old_top - new_top)
                top_ref[head] = new_top
                sum_ref[head] = sum_ref[head] * shrink + jnp.sum(weights, axis=-1, keepdims=True)
                total_ref[head] = total_ref[head] * shrink + jnp.dot(
                    weights.astype(BF16), value, preferred_element_type=F32)

    lines = total_ref.shape[1]
    places = out_ref.shape[0] * 2
    lane = lax.broadcasted_iota(jnp.int32, (lines, LANES), 1)
    notes = jnp.zeros((lines, LANES), F32)
    for head in range(HALF_HEADS):
        pieces = three_parts(top_ref[head]) + three_parts(sum_ref[head])
        for at, piece in enumerate(pieces):
            notes = jnp.where(lane == 6 * head + at, piece, notes)
        out_ref[:, :, head] = total_ref[head].astype(BF16).reshape(places // 2, 2, LINES, LANES)
    out_ref[:, :, HALF_HEADS] = notes.astype(BF16).reshape(places // 2, 2, LINES, LANES)


def cross(counts, tokens, loads, rows):
    lines = 2 * CHIPS * LINES
    sums = pltpu.VMEM((HALF_HEADS, lines, LANES), F32)
    return pl.pallas_call(
        cross_kernel,
        out_shape=jax.ShapeDtypeStruct((CHIPS, 2, HALF_HEADS + 1, LINES, LANES), BF16),
        in_specs=[SMEM] + [HBM] * 18,
        out_specs=VMEM,
        scratch_shapes=[
            pltpu.VMEM((2 * CAP, BLOCK, D_ENC), BF16),
            pltpu.VMEM((D_ENC, KV_HEADS * LANES), BF16),
            pltpu.VMEM((HALF_HEADS, lines, LANES), BF16),
            sums, sums, sums,
            pltpu.SemaphoreType.DMA((8,)), pltpu.SemaphoreType.DMA((2 * CAP,)), pltpu.SemaphoreType.DMA((16,)),
        ],
        compiler_params=pltpu.CompilerParams(vmem_limit_bytes=63 * 2**20),
        cost_estimate=pl.CostEstimate(flops=6 * 10**9, bytes_accessed=8 * 2**20, transcendentals=2**20),
    )(counts, *tokens, *loads, *rows)


def combine_kernel(*refs):
    own_ref, arrived, (keep_ref, give_ref) = refs[0], refs[1:CHIPS], refs[CHIPS:]
    me = lax.axis_index("ctx")
    core, chip = lax.rem(me, 2), me // 2
    for out_ref, part in ((keep_ref, core), (give_ref, 1 - core)):
        pieces = [own_ref.at[chip, part]] + [ref.at[part] for ref in arrived]
        notes = [piece[HALF_HEADS].astype(F32) for piece in pieces]
        for head in range(HALF_HEADS):
            at = 6 * head
            tops = [n[:, at : at + 1] + n[:, at + 1 : at + 2] + n[:, at + 2 : at + 3] for n in notes]
            sums = [n[:, at + 3 : at + 4] + n[:, at + 4 : at + 5] + n[:, at + 5 : at + 6] for n in notes]
            top = functools.reduce(jnp.maximum, tops)
            numerator, denominator = 0.0, 0.0
            for share, amount, piece in zip([jnp.exp(t - top) for t in tops], sums, pieces):
                numerator += share * piece[head].astype(F32)
                denominator += share * amount
            out_ref[head] = (numerator / denominator).astype(BF16)


def combine(own, arrived):
    shape = jax.ShapeDtypeStruct((HALF_HEADS, LINES, LANES), BF16)
    return pl.pallas_call(
        combine_kernel, out_shape=(shape, shape), in_specs=[VMEM] * CHIPS, out_specs=(VMEM, VMEM),
    )(own, *arrived)


def place_kernel(keep_ref, got_ref, out_ref):
    core = lax.rem(lax.axis_index("ctx"), 2)
    for head in range(KV_HEADS):
        mine = core == head % 2
        lines = jnp.where(mine, keep_ref[head // 2].astype(F32), got_ref[head // 2].astype(F32))
        for g in range(GROUP):
            start = (head * GROUP + g) * LANES
            out_ref[:, start : start + LANES] = lines[g * ROWS : (g + 1) * ROWS].astype(BF16)


def put_in_place(keep, got):
    return pl.pallas_call(
        place_kernel, out_shape=jax.ShapeDtypeStruct((ROWS, QW), BF16), in_specs=[VMEM] * 2, out_specs=VMEM,
    )(keep, got)


NEXT_Z = (1, 3, 0, 2)


def exchange(values, bits):
    return lax.ppermute(values, "ctx", [(i, i ^ bits) for i in range(2 * CHIPS)])


def round_z(values):
    return lax.ppermute(values, "ctx", [(i, 4 * NEXT_Z[i // 4] + i % 4) for i in range(2 * CHIPS)])


def after(values, *others):
    return lax.optimization_barrier((values,) + others)[0]


def local(context, counts, queries, norm_gain, w_query, w_key, w_value, w_out, final_gain, w_kv):
    me = lax.axis_index("ctx")
    load0 = w_kv
    load1 = round_z(load0)
    beside0 = exchange(load0, 2)
    taken = exchange(context[2], 1)
    keep, give = split_queries(queries)
    row_chip = jnp.stack([keep, exchange(give, 1)])

    cosine, sine = rotary_lanes()
    weights = (w_query, w_key, w_value, w_out, norm_gain[None], final_gain[None], cosine, sine)
    token0 = encode(0, counts, context, context, weights)
    load1, row_chip, token0, taken = lax.optimization_barrier((load1, row_chip, token0, taken))
    load2 = round_z(load1)
    beside1 = exchange(load1, 2)
    far0 = exchange(token0, 1)
    row_beside = exchange(row_chip, 2)
    token1 = encode(1, after(counts, beside0), context, taken, weights)
    load2, token1, row_beside = lax.optimization_barrier((load2, token1, row_beside))
    load3 = round_z(load2)
    beside2 = exchange(load2, 2)
    far1 = exchange(token1, 1)
    rows0 = jnp.stack([row_chip, row_beside])
    rows1 = round_z(rows0)
    token2 = encode(2, after(counts, beside1, far0), context, context, weights)
    load3, token2, rows1 = lax.optimization_barrier((load3, token2, rows1))
    beside3 = exchange(load3, 2)
    far2 = exchange(token2, 1)
    rows2 = round_z(rows1)
    rows3 = round_z(rows2)

    parts = cross(
        counts, (token0, token1, token2, far0, far1, far2),
        (load0, beside0, load1, beside1, load2, beside2, load3, beside3),
        (rows0, rows1, rows2, rows3),
    )
    arrived = [
        exchange(lax.dynamic_index_in_dim(parts, (me // 2) ^ chip, keepdims=False), 2 * chip)
        for chip in range(1, CHIPS)
    ]
    keep, give = combine(parts, arrived)
    return put_in_place(keep, exchange(give, 1))


def rotary_tables(length, head_width):
    position = jnp.arange(length).astype(jnp.float32)[:, None]
    frequency = jnp.exp(
        jnp.arange(head_width // 2).astype(jnp.float32) * (-2.0 * math.log(10000.0) / head_width)
    )
    phase_angle = position * frequency[None, :]
    return (jnp.cos(phase_angle)[:, None, :], jnp.sin(phase_angle)[:, None, :])


def rotate(values, cosine_table, sine_table):
    half_width = values.shape[-1] // 2
    lower_half = values[..., :half_width]
    upper_half = values[..., half_width:]
    return jnp.concatenate(
        [
            lower_half * cosine_table - upper_half * sine_table,
            upper_half * cosine_table + lower_half * sine_table,
        ],
        axis=-1,
    )


def weighted_sums(cross_scores, top_scores, key_alive, cross_values):
    cross_weights = jnp.where(key_alive, jnp.exp(cross_scores - top_scores[..., None]), 0.0)
    total_rows = cross_scores.shape[0]
    denominator = jnp.sum(cross_weights, axis=-1).reshape(total_rows, Q_HEADS)
    numerator = jnp.einsum(
        "rkgt,tkd->rkgd",
        cross_weights.astype(jnp.bfloat16),
        cross_values,
        preferred_element_type=jnp.float32,
    )
    return (numerator.reshape(total_rows, QW), denominator)


def local_any(context, counts, queries, norm_gain, w_query, w_key, w_value, w_out, final_gain, w_kv):
    places = lax.axis_size("ctx")
    device_index = lax.axis_index("ctx")
    device_number = jnp.arange(places)
    own_count = jnp.sum(jnp.where(device_number == device_index, counts, 0))
    alive_slot = jnp.arange(CAP) < own_count
    slot_count = context.shape[0]
    row_count = slot_count * BLOCK
    normed = root_scale(context, norm_gain).astype(jnp.bfloat16).reshape(row_count, D_ENC)
    cosine_table, sine_table = rotary_tables(BLOCK, ENC_HD)

    def project(weight):
        return jnp.dot(normed, weight, preferred_element_type=jnp.float32).reshape(
            slot_count, BLOCK, ENC_HEADS, ENC_HD
        )

    query_rows = rotate(project(w_query), cosine_table, sine_table).astype(jnp.bfloat16)
    key_rows = rotate(project(w_key), cosine_table, sine_table).astype(jnp.bfloat16)
    value_rows = project(w_value).astype(jnp.bfloat16)
    scores = jnp.einsum(
        "sqhd,skhd->shqk", query_rows, key_rows, preferred_element_type=jnp.float32
    ) / math.sqrt(ENC_HD)
    weights = jax.nn.softmax(scores, axis=-1).astype(jnp.bfloat16)
    mixed_rows = jnp.einsum(
        "shqk,skhd->sqhd", weights, value_rows, preferred_element_type=jnp.float32
    )
    mixed_rows = mixed_rows.astype(jnp.bfloat16).reshape(row_count, D_ENC)
    residual = context.reshape(row_count, D_ENC).astype(jnp.float32) + jnp.dot(
        mixed_rows, w_out, preferred_element_type=jnp.float32
    )
    final_norm = root_scale(residual, final_gain).astype(jnp.bfloat16)
    key_value = jnp.dot(
        final_norm,
        lax.all_gather(w_kv, "ctx", axis=1, tiled=True),
        preferred_element_type=jnp.float32,
    ).astype(jnp.bfloat16)
    cross_keys = key_value[:, : KV_HEADS * HEAD_DIM].reshape(row_count, KV_HEADS, HEAD_DIM)
    cross_values = key_value[:, KV_HEADS * HEAD_DIM :].reshape(row_count, KV_HEADS, HEAD_DIM)
    every_query = lax.all_gather(queries, "ctx", axis=0, tiled=True)
    total_rows = every_query.shape[0]
    grouped = every_query.reshape(total_rows, KV_HEADS, GROUP, HEAD_DIM)
    cross_scores = jnp.einsum(
        "rkgd,tkd->rkgt", grouped, cross_keys, preferred_element_type=jnp.float32
    ) / math.sqrt(HEAD_DIM)
    key_alive = jnp.repeat(alive_slot, BLOCK)
    local_top = jnp.max(jnp.where(key_alive, cross_scores, -jnp.inf), axis=-1)
    row_top = lax.pmax(local_top.astype(jnp.bfloat16), "ctx").astype(local_top.dtype)
    numerator, denominator = weighted_sums(cross_scores, row_top, key_alive, cross_values)
    own_numerator, own_denominator = (
        lax.psum_scatter(numerator, "ctx", scatter_dimension=0, tiled=True),
        lax.psum_scatter(denominator, "ctx", scatter_dimension=0, tiled=True),
    )
    own_rows = own_numerator.shape[0]
    result = own_numerator.reshape(own_rows, Q_HEADS, HEAD_DIM) / own_denominator[..., None]
    return result.reshape(own_rows, QW).astype(jnp.bfloat16)


def solution(mesh):
    in_specs = (
        P(("groups", "ctx"), None, None),
        P("groups"),
        P(("groups", "ctx"), None),
        P(),
        P(),
        P(),
        P(),
        P(),
        P(),
        P(None, "ctx"),
    )
    out_specs = P(("groups", "ctx"), None)
    small = mesh.shape["ctx"] == 2 * CHIPS
    return jax.shard_map(local if small else local_any, mesh=mesh, in_specs=in_specs, out_specs=out_specs, check_vma=False)
```

profile of v0, /device:TPU:0, one launch (start us, length us, event | category | flops | bytes accessed | tf_op | source)
XLA Modules:
  0.0 103.0 jit_solution(5620757120616498232)
XLA Ops:
  0.0 3.0 %collective-permute-start = (bf16[1024,128]{1,0:T(8,128)(2,1)}, bf16[1024,128]{1,0:T(8,128)(2,1)S(1)}, u32[]{:S(2)}, u32[]{:S(2)}) collective-permute-start(bf16[1024,128]{1,0:T(8,128)(2,1)} %refs_6_.1), channel_id=1, source_target_pairs={{0,4},{1,5},{2,6},{3,7},{4,12},{5,13},{6,14},{7,15},{8,0},{9,1},{1... | collective-permute-start | bytes 786440 | tf_op jit(solution)/shard_map/ppermute | solution.py:333
  3.0 1.5 %collective-permute-start.4 = (bf16[1024,128]{1,0:T(8,128)(2,1)}, bf16[1024,128]{1,0:T(8,128)(2,1)}, u32[]{:S(2)}, u32[]{:S(2)}) collective-permute-start(bf16[1024,128]{1,0:T(8,128)(2,1)} %refs_6_.1), channel_id=1, source_target_pairs={{0,2},{1,3},{2,0},{3,1},{4,6},{5,7},{6,4},{7,5},{8,10},{9,11},{10,... | collective-permute-start | bytes 786440 | tf_op jit(solution)/shard_map/ppermute | solution.py:329
  4.5 1.4 %shard_map.118 = (bf16[4,16,128]{2,1,0:T(8,128)(2,1)}, bf16[4,16,128]{2,1,0:T(8,128)(2,1)}) custom-call(bf16[4,4096]{1,0:T(4,128)(2,1)} %query_ref.1), custom_call_target="tpu_custom_call" | custom-call | tf_op jit(solution)/shard_map/pallas_call | solution.py:78
  8.8 1.3 %broadcast_in_dim.7.fgain_ref = bf16[1,1024]{1,0:T(2,128)(2,1)} reshape(bf16[1024]{0:T(1024)(128)(2,1)} %param.20) | data formatting | bytes 4096 | tf_op jit(solution)/shard_map/broadcast_in_dim | solution.py:350
  10.1 12.6 %shard_map.119.refs_0_ = bf16[256,1024]{1,0:T(8,128)(2,1)} custom-call(s32[16]{0:T(128)} %counts_ref.5, bf16[3,256,1024]{2,1,0:T(8,128)(2,1)} %taken_ref.3, bf16[3,256,1024]{2,1,0:T(8,128)(2,1)} %taken_ref.3, bf16[1024,1024]{1,0:T(8,128)(2,1)} %wq_ref.5, bf16[1024,1024]{1,0:T(8,128)(2,1)} %wk_ref.5, bf16[1024,1024]{1,0:T(8,128)(2,1)} %wv_ref.5, ...), custom_call_target="tpu_custom_call" | custom-call | flops 6000000000 | bytes 9437184 | tf_op jit(solution)/shard_map/pallas_call | solution.py:160
  22.8 2.6 %collective-permute-start.3 = (bf16[1024,128]{1,0:T(8,128)(2,1)S(1)}, bf16[1024,128]{1,0:T(8,128)(2,1)}, u32[]{:S(2)}, u32[]{:S(2)}) collective-permute-start(bf16[1024,128]{1,0:T(8,128)(2,1)S(1)} %collective-permute-done.refs_8_), channel_id=1, source_target_pairs={{0,4},{1,5},{2,6},{3,7},{4,12},{5,13},{6,14},{7,15},{8,0},{9,1},{1... | collective-permute-start | bytes 786440 | tf_op jit(solution)/shard_map/ppermute | solution.py:333
  25.9 1.5 %collective-permute-start.5 = (bf16[2,4,16,128]{3,2,1,0:T(8,128)(2,1)S(1)}, bf16[2,4,16,128]{3,2,1,0:T(8,128)(2,1)S(1)}, u32[]{:S(2)}, u32[]{:S(2)}) collective-permute-start(bf16[2,4,16,128]{3,2,1,0:T(8,128)(2,1)S(1)} %pad_maximum_fusion.1), channel_id=1, source_target_pairs={{0,2},{1,3},{2,0},{3,1},{4,6},{5,7},{6,4},{7,5},{8,10},{9,11},{10,... | collective-permute-start | bytes 98312 | tf_op jit(solution)/shard_map/ppermute | solution.py:329
  27.5 12.6 %shard_map.120.refs_1_ = bf16[256,1024]{1,0:T(8,128)(2,1)} custom-call(s32[16]{0:T(128)} %counts_ref.5, bf16[3,256,1024]{2,1,0:T(8,128)(2,1)} %taken_ref.3, bf16[256,1024]{1,0:T(8,128)(2,1)} %collective-permute-done.2.taken_ref, bf16[1024,1024]{1,0:T(8,128)(2,1)} %wq_ref.5, bf16[1024,1024]{1,0:T(8,128)(2,1)} %wk_ref.5, bf16[1024,1024]{1,0:T(8,128)(2,1)} %wv_ref.5, ...), custom_call_target="tpu_custom_call" | custom-call | flops 6000000000 | bytes 9437184 | tf_op jit(solution)/shard_map/pallas_call | solution.py:160
  41.0 2.4 %shard_map.121.refs_2_ = bf16[256,1024]{1,0:T(8,128)(2,1)} custom-call(s32[16]{0:T(128)} %counts_ref.5, bf16[3,256,1024]{2,1,0:T(8,128)(2,1)} %taken_ref.3, bf16[3,256,1024]{2,1,0:T(8,128)(2,1)} %taken_ref.3, bf16[1024,1024]{1,0:T(8,128)(2,1)} %wq_ref.5, bf16[1024,1024]{1,0:T(8,128)(2,1)} %wk_ref.5, bf16[1024,1024]{1,0:T(8,128)(2,1)} %wv_ref.5, ...), custom_call_target="tpu_custom_call" | custom-call | flops 6000000000 | bytes 9437184 | tf_op jit(solution)/shard_map/pallas_call | solution.py:160
  43.4 2.6 %collective-permute-done.9.refs_15_ = bf16[2,2,4,16,128]{4,3,2,1,0:T(8,128)(2,1)S(1)} collective-permute-done((bf16[2,2,4,16,128]{4,3,2,1,0:T(8,128)(2,1)S(1)}, bf16[2,2,4,16,128]{4,3,2,1,0:T(8,128)(2,1)S(1)}, u32[]{:S(2)}, u32[]{:S(2)}) %collective-permute-start.9) | collective-permute-done | bytes 65568 | tf_op jit(solution)/shard_map/ppermute | solution.py:333
  46.0 5.4 %collective-permute-done.6.refs_12_ = bf16[1024,128]{1,0:T(8,128)(2,1)} collective-permute-done((bf16[1024,128]{1,0:T(8,128)(2,1)}, bf16[1024,128]{1,0:T(8,128)(2,1)}, u32[]{:S(2)}, u32[]{:S(2)}) %collective-permute-start.6) | collective-permute-done | bytes 262176 | tf_op jit(solution)/shard_map/ppermute | solution.py:333
  51.5 2.0 %collective-permute-start.13 = (bf16[1024,128]{1,0:T(8,128)(2,1)}, bf16[1024,128]{1,0:T(8,128)(2,1)S(1)}, u32[]{:S(2)}, u32[]{:S(2)}) collective-permute-start(bf16[1024,128]{1,0:T(8,128)(2,1)} %collective-permute-done.6.refs_12_), channel_id=1, source_target_pairs={{0,2},{1,3},{2,0},{3,1},{4,6},{5,7},{6,4},{7,5},{8,10},{9,11},{10,... | collective-permute-start | bytes 786440 | tf_op jit(solution)/shard_map/ppermute | solution.py:329
  53.5 5.2 %collective-permute-done.14.refs_16_ = bf16[2,2,4,16,128]{4,3,2,1,0:T(8,128)(2,1)S(1)} collective-permute-done((bf16[2,2,4,16,128]{4,3,2,1,0:T(8,128)(2,1)S(1)}, bf16[2,2,4,16,128]{4,3,2,1,0:T(8,128)(2,1)S(1)}, u32[]{:S(2)}, u32[]{:S(2)}) %collective-permute-start.14) | collective-permute-done | bytes 65568 | tf_op jit(solution)/shard_map/ppermute | solution.py:333
  58.7 2.1 %collective-permute-done.12.refs_11_ = bf16[1024,128]{1,0:T(8,128)(2,1)S(1)} collective-permute-done((bf16[1024,128]{1,0:T(8,128)(2,1)}, bf16[1024,128]{1,0:T(8,128)(2,1)S(1)}, u32[]{:S(2)}, u32[]{:S(2)}) %collective-permute-start.12) | collective-permute-done | bytes 262176 | tf_op jit(solution)/shard_map/ppermute | solution.py:329
  60.8 3.0 %collective-permute-done.15.refs_17_ = bf16[2,2,4,16,128]{4,3,2,1,0:T(8,128)(2,1)S(1)} collective-permute-done((bf16[2,2,4,16,128]{4,3,2,1,0:T(8,128)(2,1)S(1)}, bf16[2,2,4,16,128]{4,3,2,1,0:T(8,128)(2,1)S(1)}, u32[]{:S(2)}, u32[]{:S(2)}) %collective-permute-start.15) | collective-permute-done | bytes 65568 | tf_op jit(solution)/shard_map/ppermute | solution.py:333
  63.8 2.2 %collective-permute-done.13.refs_13_ = bf16[1024,128]{1,0:T(8,128)(2,1)S(1)} collective-permute-done((bf16[1024,128]{1,0:T(8,128)(2,1)}, bf16[1024,128]{1,0:T(8,128)(2,1)S(1)}, u32[]{:S(2)}, u32[]{:S(2)}) %collective-permute-start.13) | collective-permute-done | bytes 262176 | tf_op jit(solution)/shard_map/ppermute | solution.py:329
  67.6 14.6 %shard_map.122.refs_0_ = bf16[8,2,5,16,128]{4,3,2,1,0:T(8,128)(2,1)} custom-call(s32[16]{0:T(128)} %counts_ref.5, bf16[256,1024]{1,0:T(8,128)(2,1)} %shard_map.119.refs_0_, bf16[256,1024]{1,0:T(8,128)(2,1)} %shard_map.120.refs_1_, bf16[256,1024]{1,0:T(8,128)(2,1)} %shard_map.121.refs_2_, bf16[256,1024]{1,0:T(8,128)(2,1)} %copy-done.10, ...), custom_call_target="tpu_custom_call" | custom-call | flops 6000000000 | bytes 8388608 | tf_op jit(solution)/shard_map/pallas_call | solution.py:266
  83.3 3.4 %collective-permute-start.18 = (bf16[2,5,16,128]{3,2,1,0:T(8,128)(2,1)S(1)}, bf16[2,5,16,128]{3,2,1,0:T(8,128)(2,1)S(1)}, u32[]{:S(2)}, u32[]{:S(2)}) collective-permute-start(bf16[2,5,16,128]{3,2,1,0:T(8,128)(2,1)S(1)} %get-tuple-element.41), channel_id=1, source_target_pairs={{0,6},{1,7},{2,4},{3,5},{4,2},{5,3},{6,0},{7,1},{8,14},{9,15},{10,... | collective-permute-start | bytes 122888 | tf_op jit(solution)/shard_map/ppermute | solution.py:329
  86.7 2.4 %collective-permute-start.20 = (bf16[2,5,16,128]{3,2,1,0:T(8,128)(2,1)S(1)}, bf16[2,5,16,128]{3,2,1,0:T(8,128)(2,1)S(1)}, u32[]{:S(2)}, u32[]{:S(2)}) collective-permute-start(bf16[2,5,16,128]{3,2,1,0:T(8,128)(2,1)S(1)} %get-tuple-element.39), channel_id=1, source_target_pairs={{0,10},{1,11},{2,8},{3,9},{4,14},{5,15},{6,12},{7,13},{8,2},{9,3},... | collective-permute-start | bytes 122888 | tf_op jit(solution)/shard_map/ppermute | solution.py:329
  89.2 5.2 %collective-permute-start.22 = (bf16[2,5,16,128]{3,2,1,0:T(8,128)(2,1)S(1)}, bf16[2,5,16,128]{3,2,1,0:T(8,128)(2,1)S(1)}, u32[]{:S(2)}, u32[]{:S(2)}) collective-permute-start(bf16[2,5,16,128]{3,2,1,0:T(8,128)(2,1)S(1)} %get-tuple-element.37), channel_id=1, source_target_pairs={{0,14},{1,15},{2,12},{3,13},{4,10},{5,11},{6,8},{7,9},{8,6},{9,7},... | collective-permute-start | bytes 122888 | tf_op jit(solution)/shard_map/ppermute | solution.py:329
  95.1 1.7 %collective-permute-done.22.refs_7_ = bf16[2,5,16,128]{3,2,1,0:T(8,128)(2,1)S(1)} collective-permute-done((bf16[2,5,16,128]{3,2,1,0:T(8,128)(2,1)S(1)}, bf16[2,5,16,128]{3,2,1,0:T(8,128)(2,1)S(1)}, u32[]{:S(2)}, u32[]{:S(2)}) %collective-permute-start.22) | collective-permute-done | bytes 40992 | tf_op jit(solution)/shard_map/ppermute | solution.py:329
  97.5 2.2 %shard_map.123 = (bf16[4,16,128]{2,1,0:T(8,128)(2,1)}, bf16[4,16,128]{2,1,0:T(8,128)(2,1)}) custom-call(bf16[8,2,5,16,128]{4,3,2,1,0:T(8,128)(2,1)} %shard_map.122.refs_0_, bf16[2,5,16,128]{3,2,1,0:T(8,128)(2,1)} %copy-done.1, bf16[2,5,16,128]{3,2,1,0:T(8,128)(2,1)} %copy-done.2, bf16[2,5,16,128]{3,2,1,0:T(8,128)(2,1)} %copy-done.3, ...), custom_call_target="tpu_custom_call" | custom-call | tf_op jit(solution)/shard_map/pallas_call | solution.py:304
  99.6 1.4 %collective-permute-done.23.got_ref = bf16[4,16,128]{2,1,0:T(8,128)(2,1)S(1)} collective-permute-done((bf16[4,16,128]{2,1,0:T(8,128)(2,1)}, bf16[4,16,128]{2,1,0:T(8,128)(2,1)S(1)}, u32[]{:S(2)}, u32[]{:S(2)}) %collective-permute-start.23) | collective-permute-done | bytes 16416 | tf_op jit(solution)/shard_map/ppermute | solution.py:329
  101.6 1.4 %shard_map.124 = bf16[4,4096]{1,0:T(4,128)(2,1)} custom-call(bf16[4,16,128]{2,1,0:T(8,128)(2,1)} %get-tuple-element.35.keep_ref, bf16[4,16,128]{2,1,0:T(8,128)(2,1)} %copy-done.9), custom_call_target="tpu_custom_call" | custom-call | tf_op jit(solution)/shard_map/pallas_call | solution.py:320
  (73 shorter events, 8.9 us)
Async XLA Ops:
  0.0 22.8 %collective-permute-start = (bf16[1024,128]{1,0:T(8,128)(2,1)}, bf16[1024,128]{1,0:T(8,128)(2,1)S(1)}, u32[]{:S(2)}, u32[]{:S(2)}) collective-permute-start(bf16[1024,128]{1,0:T(8,128)(2,1)} %refs_6_.1), channel_id=1, source_target_pairs={{0,4},{1,5},{2,6},{3,7},{4,12},{5,13},{6,14},{7,15},{8,0},{9,1},{1... | collective-permute-start | bytes 786440 | tf_op jit(solution)/shard_map/ppermute | solution.py:333
  3.0 19.7 %collective-permute-start.4 = (bf16[1024,128]{1,0:T(8,128)(2,1)}, bf16[1024,128]{1,0:T(8,128)(2,1)}, u32[]{:S(2)}, u32[]{:S(2)}) collective-permute-start(bf16[1024,128]{1,0:T(8,128)(2,1)} %refs_6_.1), channel_id=1, source_target_pairs={{0,2},{1,3},{2,0},{3,1},{4,6},{5,7},{6,4},{7,5},{8,10},{9,11},{10,... | collective-permute-start | bytes 786440 | tf_op jit(solution)/shard_map/ppermute | solution.py:329
  5.9 16.8 %collective-permute-start.1 = (bf16[4,16,128]{2,1,0:T(8,128)(2,1)}, bf16[4,16,128]{2,1,0:T(8,128)(2,1)S(1)}, u32[]{:S(2)}, u32[]{:S(2)}) collective-permute-start(bf16[4,16,128]{2,1,0:T(8,128)(2,1)} %get-tuple-element.22), channel_id=1, source_target_pairs={{0,1},{1,0},{2,3},{3,2},{4,5},{5,4},{6,7},{7,6},{8,9},{9,8},{10,11... | collective-permute-start | bytes 49160 | tf_op jit(solution)/shard_map/ppermute | solution.py:329
  7.0 15.8 %collective-permute-start.2 = (bf16[256,1024]{1,0:T(8,128)(2,1)S(1)}, bf16[256,1024]{1,0:T(8,128)(2,1)}, u32[]{:S(2)}, u32[]{:S(2)}) collective-permute-start(bf16[256,1024]{1,0:T(8,128)(2,1)S(1)} %slice_bitcast_fusion), channel_id=1, source_target_pairs={{0,1},{1,0},{2,3},{3,2},{4,5},{5,4},{6,7},{7,6},{8,9},{9,8},{10,11... | collective-permute-start | bytes 1572872 | tf_op jit(solution)/shard_map/ppermute | solution.py:329
  22.8 17.3 %collective-permute-start.3 = (bf16[1024,128]{1,0:T(8,128)(2,1)S(1)}, bf16[1024,128]{1,0:T(8,128)(2,1)}, u32[]{:S(2)}, u32[]{:S(2)}) collective-permute-start(bf16[1024,128]{1,0:T(8,128)(2,1)S(1)} %collective-permute-done.refs_8_), channel_id=1, source_target_pairs={{0,4},{1,5},{2,6},{3,7},{4,12},{5,13},{6,14},{7,15},{8,0},{9,1},{1... | collective-permute-start | bytes 786440 | tf_op jit(solution)/shard_map/ppermute | solution.py:333
  25.4 15.6 %collective-permute-start.7 = (bf16[1024,128]{1,0:T(8,128)(2,1)S(1)}, bf16[1024,128]{1,0:T(8,128)(2,1)}, u32[]{:S(2)}, u32[]{:S(2)}) collective-permute-start(bf16[1024,128]{1,0:T(8,128)(2,1)S(1)} %collective-permute-done.refs_8_), channel_id=1, source_target_pairs={{0,2},{1,3},{2,0},{3,1},{4,6},{5,7},{6,4},{7,5},{8,10},{9,11},{10,... | collective-permute-start | bytes 786440 | tf_op jit(solution)/shard_map/ppermute | solution.py:329
  25.9 14.1 %collective-permute-start.5 = (bf16[2,4,16,128]{3,2,1,0:T(8,128)(2,1)S(1)}, bf16[2,4,16,128]{3,2,1,0:T(8,128)(2,1)S(1)}, u32[]{:S(2)}, u32[]{:S(2)}) collective-permute-start(bf16[2,4,16,128]{3,2,1,0:T(8,128)(2,1)S(1)} %pad_maximum_fusion.1), channel_id=1, source_target_pairs={{0,2},{1,3},{2,0},{3,1},{4,6},{5,7},{6,4},{7,5},{8,10},{9,11},{10,... | collective-permute-start | bytes 98312 | tf_op jit(solution)/shard_map/ppermute | solution.py:329
  27.4 13.6 %collective-permute-start.8 = (bf16[256,1024]{1,0:T(8,128)(2,1)}, bf16[256,1024]{1,0:T(8,128)(2,1)S(1)}, u32[]{:S(2)}, u32[]{:S(2)}) collective-permute-start(bf16[256,1024]{1,0:T(8,128)(2,1)} %shard_map.119.refs_0_), channel_id=1, source_target_pairs={{0,1},{1,0},{2,3},{3,2},{4,5},{5,4},{6,7},{7,6},{8,9},{9,8},{10,11... | collective-permute-start | bytes 1572872 | tf_op jit(solution)/shard_map/ppermute | solution.py:329
  40.1 5.9 %collective-permute-start.9 = (bf16[2,2,4,16,128]{4,3,2,1,0:T(8,128)(2,1)S(1)}, bf16[2,2,4,16,128]{4,3,2,1,0:T(8,128)(2,1)S(1)}, u32[]{:S(2)}, u32[]{:S(2)}) collective-permute-start(bf16[2,2,4,16,128]{4,3,2,1,0:T(8,128)(2,1)S(1)} %pad_maximum_fusion.refs_14_), channel_id=1, source_target_pairs={{0,4},{1,5},{2,6},{3,7},{4,12},{5,13},{6,14},{7,15},{8,0},{9,1},{1... | collective-permute-start | bytes 196616 | tf_op jit(solution)/shard_map/ppermute | solution.py:333
  40.2 11.3 %collective-permute-start.6 = (bf16[1024,128]{1,0:T(8,128)(2,1)}, bf16[1024,128]{1,0:T(8,128)(2,1)}, u32[]{:S(2)}, u32[]{:S(2)}) collective-permute-start(bf16[1024,128]{1,0:T(8,128)(2,1)} %collective-permute-done.3.refs_10_), channel_id=1, source_target_pairs={{0,4},{1,5},{2,6},{3,7},{4,12},{5,13},{6,14},{7,15},{8,0},{9,1},{1... | collective-permute-start | bytes 786440 | tf_op jit(solution)/shard_map/ppermute | solution.py:333
  40.3 26.5 %collective-permute-start.10 = (bf16[256,1024]{1,0:T(8,128)(2,1)}, bf16[256,1024]{1,0:T(8,128)(2,1)}, u32[]{:S(2)}, u32[]{:S(2)}) collective-permute-start(bf16[256,1024]{1,0:T(8,128)(2,1)} %shard_map.120.refs_1_), channel_id=1, source_target_pairs={{0,1},{1,0},{2,3},{3,2},{4,5},{5,4},{6,7},{7,6},{8,9},{9,8},{10,11... | collective-permute-start | bytes 1572872 | tf_op jit(solution)/shard_map/ppermute | solution.py:329
  51.5 15.3 %collective-permute-start.11 = (bf16[256,1024]{1,0:T(8,128)(2,1)}, bf16[256,1024]{1,0:T(8,128)(2,1)S(1)}, u32[]{:S(2)}, u32[]{:S(2)}) collective-permute-start(bf16[256,1024]{1,0:T(8,128)(2,1)} %shard_map.121.refs_2_), channel_id=1, source_target_pairs={{0,1},{1,0},{2,3},{3,2},{4,5},{5,4},{6,7},{7,6},{8,9},{9,8},{10,11... | collective-permute-start | bytes 1572872 | tf_op jit(solution)/shard_map/ppermute | solution.py:329
  51.5 9.3 %collective-permute-start.12 = (bf16[1024,128]{1,0:T(8,128)(2,1)}, bf16[1024,128]{1,0:T(8,128)(2,1)S(1)}, u32[]{:S(2)}, u32[]{:S(2)}) collective-permute-start(bf16[1024,128]{1,0:T(8,128)(2,1)} %collective-permute-done.3.refs_10_), channel_id=1, source_target_pairs={{0,2},{1,3},{2,0},{3,1},{4,6},{5,7},{6,4},{7,5},{8,10},{9,11},{10,... | collective-permute-start | bytes 786440 | tf_op jit(solution)/shard_map/ppermute | solution.py:329
  51.5 14.5 %collective-permute-start.13 = (bf16[1024,128]{1,0:T(8,128)(2,1)}, bf16[1024,128]{1,0:T(8,128)(2,1)S(1)}, u32[]{:S(2)}, u32[]{:S(2)}) collective-permute-start(bf16[1024,128]{1,0:T(8,128)(2,1)} %collective-permute-done.6.refs_12_), channel_id=1, source_target_pairs={{0,2},{1,3},{2,0},{3,1},{4,6},{5,7},{6,4},{7,5},{8,10},{9,11},{10,... | collective-permute-start | bytes 786440 | tf_op jit(solution)/shard_map/ppermute | solution.py:329
  53.5 5.2 %collective-permute-start.14 = (bf16[2,2,4,16,128]{4,3,2,1,0:T(8,128)(2,1)S(1)}, bf16[2,2,4,16,128]{4,3,2,1,0:T(8,128)(2,1)S(1)}, u32[]{:S(2)}, u32[]{:S(2)}) collective-permute-start(bf16[2,2,4,16,128]{4,3,2,1,0:T(8,128)(2,1)S(1)} %collective-permute-done.9.refs_15_), channel_id=1, source_target_pairs={{0,4},{1,5},{2,6},{3,7},{4,12},{5,13},{6,14},{7,15},{8,0},{9,1},{1... | collective-permute-start | bytes 196616 | tf_op jit(solution)/shard_map/ppermute | solution.py:333
  58.7 5.2 %collective-permute-start.15 = (bf16[2,2,4,16,128]{4,3,2,1,0:T(8,128)(2,1)S(1)}, bf16[2,2,4,16,128]{4,3,2,1,0:T(8,128)(2,1)S(1)}, u32[]{:S(2)}, u32[]{:S(2)}) collective-permute-start(bf16[2,2,4,16,128]{4,3,2,1,0:T(8,128)(2,1)S(1)} %collective-permute-done.14.refs_16_), channel_id=1, source_target_pairs={{0,4},{1,5},{2,6},{3,7},{4,12},{5,13},{6,14},{7,15},{8,0},{9,1},{1... | collective-permute-start | bytes 196616 | tf_op jit(solution)/shard_map/ppermute | solution.py:333
  83.2 6.0 %collective-permute-start.16 = (bf16[2,5,16,128]{3,2,1,0:T(8,128)(2,1)S(1)}, bf16[2,5,16,128]{3,2,1,0:T(8,128)(2,1)S(1)}, u32[]{:S(2)}, u32[]{:S(2)}) collective-permute-start(bf16[2,5,16,128]{3,2,1,0:T(8,128)(2,1)S(1)} %get-tuple-element.43), channel_id=1, source_target_pairs={{0,2},{1,3},{2,0},{3,1},{4,6},{5,7},{6,4},{7,5},{8,10},{9,11},{10,... | collective-permute-start | bytes 122888 | tf_op jit(solution)/shard_map/ppermute | solution.py:329
  83.3 5.9 %collective-permute-start.17 = (bf16[2,5,16,128]{3,2,1,0:T(8,128)(2,1)S(1)}, bf16[2,5,16,128]{3,2,1,0:T(8,128)(2,1)S(1)}, u32[]{:S(2)}, u32[]{:S(2)}) collective-permute-start(bf16[2,5,16,128]{3,2,1,0:T(8,128)(2,1)S(1)} %get-tuple-element.42), channel_id=1, source_target_pairs={{0,4},{1,5},{2,6},{3,7},{4,0},{5,1},{6,2},{7,3},{8,12},{9,13},{10,... | collective-permute-start | bytes 122888 | tf_op jit(solution)/shard_map/ppermute | solution.py:329
  83.3 11.1 %collective-permute-start.18 = (bf16[2,5,16,128]{3,2,1,0:T(8,128)(2,1)S(1)}, bf16[2,5,16,128]{3,2,1,0:T(8,128)(2,1)S(1)}, u32[]{:S(2)}, u32[]{:S(2)}) collective-permute-start(bf16[2,5,16,128]{3,2,1,0:T(8,128)(2,1)S(1)} %get-tuple-element.41), channel_id=1, source_target_pairs={{0,6},{1,7},{2,4},{3,5},{4,2},{5,3},{6,0},{7,1},{8,14},{9,15},{10,... | collective-permute-start | bytes 122888 | tf_op jit(solution)/shard_map/ppermute | solution.py:329
  86.7 7.7 %collective-permute-start.19 = (bf16[2,5,16,128]{3,2,1,0:T(8,128)(2,1)S(1)}, bf16[2,5,16,128]{3,2,1,0:T(8,128)(2,1)S(1)}, u32[]{:S(2)}, u32[]{:S(2)}) collective-permute-start(bf16[2,5,16,128]{3,2,1,0:T(8,128)(2,1)S(1)} %get-tuple-element.40), channel_id=1, source_target_pairs={{0,8},{1,9},{2,10},{3,11},{4,12},{5,13},{6,14},{7,15},{8,0},{9,1},... | collective-permute-start | bytes 122888 | tf_op jit(solution)/shard_map/ppermute | solution.py:329
  86.7 7.7 %collective-permute-start.20 = (bf16[2,5,16,128]{3,2,1,0:T(8,128)(2,1)S(1)}, bf16[2,5,16,128]{3,2,1,0:T(8,128)(2,1)S(1)}, u32[]{:S(2)}, u32[]{:S(2)}) collective-permute-start(bf16[2,5,16,128]{3,2,1,0:T(8,128)(2,1)S(1)} %get-tuple-element.39), channel_id=1, source_target_pairs={{0,10},{1,11},{2,8},{3,9},{4,14},{5,15},{6,12},{7,13},{8,2},{9,3},... | collective-permute-start | bytes 122888 | tf_op jit(solution)/shard_map/ppermute | solution.py:329
  89.2 5.9 %collective-permute-start.21 = (bf16[2,5,16,128]{3,2,1,0:T(8,128)(2,1)S(1)}, bf16[2,5,16,128]{3,2,1,0:T(8,128)(2,1)S(1)}, u32[]{:S(2)}, u32[]{:S(2)}) collective-permute-start(bf16[2,5,16,128]{3,2,1,0:T(8,128)(2,1)S(1)} %get-tuple-element.38), channel_id=1, source_target_pairs={{0,12},{1,13},{2,14},{3,15},{4,8},{5,9},{6,10},{7,11},{8,4},{9,5},... | collective-permute-start | bytes 122888 | tf_op jit(solution)/shard_map/ppermute | solution.py:329
  89.2 7.6 %collective-permute-start.22 = (bf16[2,5,16,128]{3,2,1,0:T(8,128)(2,1)S(1)}, bf16[2,5,16,128]{3,2,1,0:T(8,128)(2,1)S(1)}, u32[]{:S(2)}, u32[]{:S(2)}) collective-permute-start(bf16[2,5,16,128]{3,2,1,0:T(8,128)(2,1)S(1)} %get-tuple-element.37), channel_id=1, source_target_pairs={{0,14},{1,15},{2,12},{3,13},{4,10},{5,11},{6,8},{7,9},{8,6},{9,7},... | collective-permute-start | bytes 122888 | tf_op jit(solution)/shard_map/ppermute | solution.py:329
  99.6 1.4 %collective-permute-start.23 = (bf16[4,16,128]{2,1,0:T(8,128)(2,1)}, bf16[4,16,128]{2,1,0:T(8,128)(2,1)S(1)}, u32[]{:S(2)}, u32[]{:S(2)}) collective-permute-start(bf16[4,16,128]{2,1,0:T(8,128)(2,1)} %get-tuple-element.36), channel_id=1, source_target_pairs={{0,1},{1,0},{2,3},{3,2},{4,5},{5,4},{6,7},{7,6},{8,9},{9,8},{10,11... | collective-permute-start | bytes 49160 | tf_op jit(solution)/shard_map/ppermute | solution.py:329
  (18 other events, 100.3 us)
where the time goes:
time: 103 us
  Pallas kernels  47.1 us (46%)
  waiting for transfers between devices  24.3 us (24%)
  starting transfers between devices  23.8 us (23%)
  local copies, waits for them, and re-layouts  7.33 us (7%)
    pallas_call x3, Pallas kernels, encode(): pl.pallas_call(functools.partial(encoder_kernel, slot), out_shape=jax.Sha...  27.6 us
    ppermute x18, starting transfers between devices, exchange(): lax.ppermute(values, 'ctx', [(i, i ^ bits) for i in range(2 * CHIPS)])  18.1 us
    ppermute x6, waiting for transfers between devices, round_z(): lax.ppermute(values, 'ctx', [(i, 4 * NEXT_Z[i // 4] + i % 4) for i in ran...  16.3 us
    pallas_call x1, Pallas kernels, cross(): pl.pallas_call(cross_kernel, out_shape=jax.ShapeDtypeStruct((CHIPS, 2, HA...  14.6 us
    ppermute x18, waiting for transfers between devices, exchange(): lax.ppermute(values, 'ctx', [(i, i ^ bits) for i in range(2 * CHIPS)])  8.09 us
    ppermute x6, starting transfers between devices, round_z(): lax.ppermute(values, 'ctx', [(i, 4 * NEXT_Z[i // 4] + i % 4) for i in ran...  5.78 us
    unnamed x36, local copies, waits for them, and re-layouts  2.78 us
    pallas_call x1, Pallas kernels, combine(): pl.pallas_call(combine_kernel, out_shape=(shape, shape), in_specs=[VMEM]...  2.17 us
  transfers between devices with their start and end apart: 24, of which 9 were waited for; matrix products, arithmetic and copies ran while one was open for 4% of the time, Pallas kernels for 28%

commit v1 on v0

--- a/solution.py
+++ b/solution.py
@@ -47,10 +47,10 @@
     frequency = 10000.0 ** (-2.0 * np.arange(ENC_HD // 2) / ENC_HD)
     angle = position * frequency[None, :]
     cosine, sine = np.cos(angle), np.sin(angle)
-    return (
-        jnp.asarray(np.concatenate([cosine, cosine, cosine, cosine], axis=1), F32),
-        jnp.asarray(np.concatenate([-sine, sine, -sine, sine], axis=1), F32),
-    )
+    return jnp.asarray(np.stack([
+        np.concatenate([cosine, cosine, cosine, cosine], axis=1),
+        np.concatenate([-sine, sine, -sine, sine], axis=1),
+    ]), F32)
 
 
 def live_counts(counts_ref):
@@ -61,7 +61,7 @@
     return own - gives + takes, other + gives - takes, takes
 
 
-def query_kernel(query_ref, keep_ref, give_ref):
+def split_rows(query_ref, keep_ref, give_ref):
     core = lax.rem(lax.axis_index("ctx"), 2)
     width = GROUP * HEAD_DIM
     for out_ref, parity in ((keep_ref, core), (give_ref, 1 - core)):
@@ -73,103 +73,103 @@
             ).astype(BF16)
 
 
-def split_queries(queries):
-    shape = jax.ShapeDtypeStruct((HALF_HEADS, LINES, LANES), BF16)
-    return pl.pallas_call(
-        query_kernel, out_shape=(shape, shape), in_specs=[VMEM], out_specs=(VMEM, VMEM),
-    )(queries)
-
-
-def encoder_kernel(slot, counts_ref, context_ref, taken_ref, wq_ref, wk_ref, wv_ref, wo_ref, gain_ref, fgain_ref,
-                   cos_ref, sin_ref, out_ref, mixed_ref, x_ref, q_buf, k_buf, v_buf, o_buf, sems, x_sem):
+def encoder_kernel(slot, counts_ref, context_ref, taken_ref, wq_ref, wk_ref, wv_ref, wo_ref, table_ref, gain_ref,
+                   fgain_ref, *refs):
+    rows_in, refs = refs[: 2 if slot else 1], refs[2 if slot else 1 :]
+    out_ref, refs = refs[0], refs[1:]
+    rows_out, refs = refs[: 1 if slot else 2], refs[1 if slot else 2 :]
+    mixed_ref, x_ref, q_ref, k_ref, v_ref, final_ref, table_buf, q_buf, k_buf, v_buf, o_buf, sems = refs
     live, _, takes = live_counts(counts_ref)
+    copies = [
+        pltpu.make_async_copy(hbm, buf, sems.at[at])
+        for at, (hbm, buf) in enumerate(
+            ((context_ref.at[slot], x_ref), (wq_ref, q_buf), (table_ref, table_buf), (wk_ref, k_buf),
+             (wv_ref, v_buf), (wo_ref, o_buf)))
+    ]
 
     @pl.when(live > slot)
     def _():
         if slot == 1:
             @pl.when(takes != 0)
             def _():
-                pltpu.make_async_copy(taken_ref, x_ref, x_sem).start()
+                pltpu.make_async_copy(taken_ref.at[CAP - 1], x_ref, sems.at[0]).start()
 
             @pl.when(takes == 0)
             def _():
-                pltpu.make_async_copy(context_ref.at[slot], x_ref, x_sem).start()
+                copies[0].start()
         else:
-            pltpu.make_async_copy(context_ref.at[slot], x_ref, x_sem).start()
-
-        copies = []
-        for part in range(PARTS):
-            columns = slice(part * PART, (part + 1) * PART)
-            copies.append([
-                pltpu.make_async_copy(hbm.at[:, columns], buf.at[:, columns], sems.at[part, at])
-                for at, (hbm, buf) in enumerate(((wq_ref, q_buf), (wk_ref, k_buf), (wv_ref, v_buf)))
-            ])
-        for group in copies:
-            for copy in group:
-                copy.start()
-        out_copy = pltpu.make_async_copy(wo_ref, o_buf, sems.at[0, 3])
-        out_copy.start()
-        pltpu.make_async_copy(context_ref.at[slot], x_ref, x_sem).wait()
-
+            copies[0].start()
+        for copy in copies[1:]:
+            copy.start()
+
+    if slot == 0:
+        split_rows(rows_in[0], rows_out[0], rows_out[1])
+    else:
+        rows_out[0][0] = rows_in[0][...]
+        rows_out[0][1] = rows_in[1][...]
+
+    @pl.when(live > slot)
+    def _():
+        copies[0].wait()
         normed = root_scale(x_ref[...], gain_ref[...]).astype(BF16)
-        cosine, sine = cos_ref[...], sin_ref[...]
-        cosine_query, sine_query = cosine * 0.125, sine * 0.125
+        copies[1].wait()
+        copies[2].wait()
+        cosine, sine = table_buf[0], table_buf[1]
         lane = lax.broadcasted_iota(jnp.int32, (BLOCK, LANES), 1)
         lower = (lane % ENC_HD) < ENC_HD // 2
         first = lane < ENC_HD
 
-        def rotate(values, cosine, sine):
-            swapped = jnp.where(
-                lower,
-                pltpu.roll(values, LANES - ENC_HD // 2, 1),
-                pltpu.roll(values, ENC_HD // 2, 1),
-            )
-            return (values * cosine + swapped * sine).astype(BF16)
-
-        for part in range(PARTS):
-            columns = slice(part * PART, (part + 1) * PART)
-            for copy in copies[part]:
-                copy.wait()
-            query = jnp.dot(normed, q_buf[:, columns], preferred_element_type=F32)
-            key = jnp.dot(normed, k_buf[:, columns], preferred_element_type=F32)
-            value = jnp.dot(normed, v_buf[:, columns], preferred_element_type=F32).astype(BF16)
-            for pair in range(PART // LANES):
-                cut = slice(pair * LANES, (pair + 1) * LANES)
-                query_pair = rotate(query[:, cut], cosine_query, sine_query)
-                key_pair = rotate(key[:, cut], cosine, sine)
-                value_pair = value[:, cut]
-                mixed = []
-                for head in range(2):
-                    own = first if head == 0 else jnp.logical_not(first)
-                    scores = lax.dot_general(
-                        jnp.where(own, query_pair, jnp.zeros_like(query_pair)), key_pair,
-                        (((1,), (1,)), ((), ())), preferred_element_type=F32,
-                    )
-                    weights = jnp.exp(scores - jnp.max(scores, axis=-1, keepdims=True))
-                    weights = weights * (1.0 / jnp.sum(weights, axis=-1, keepdims=True))
-                    mixed.append(jnp.dot(weights.astype(BF16), value_pair, preferred_element_type=F32))
-                start = part * PART + pair * LANES
-                mixed_ref[:, start : start + LANES] = jnp.where(first, mixed[0], mixed[1]).astype(BF16)
-        out_copy.wait()
+        def project(buf, to_ref, cosine, sine):
+            for part in range(PARTS):
+                values = jnp.dot(normed, buf[:, part * PART : (part + 1) * PART], preferred_element_type=F32)
+                for at in range(PART // LANES):
+                    cut = values[:, at * LANES : (at + 1) * LANES]
+                    swapped = jnp.where(
+                        lower, pltpu.roll(cut, LANES - ENC_HD // 2, 1), pltpu.roll(cut, ENC_HD // 2, 1))
+                    start = part * PART + at * LANES
+                    to_ref[:, start : start + LANES] = (cut * cosine + swapped * sine).astype(BF16)
+
+        project(q_buf, q_ref, cosine * 0.125, sine * 0.125)
+        copies[3].wait()
+        project(k_buf, k_ref, cosine, sine)
+        copies[4].wait()
+        v_ref[...] = jnp.dot(normed, v_buf[...], preferred_element_type=F32).astype(BF16)
+        for pair in range(ENC_HEADS // 2):
+            cut = slice(pair * LANES, (pair + 1) * LANES)
+            query, key, value = q_ref[:, cut], k_ref[:, cut], v_ref[:, cut]
+            mixed = []
+            for own in (first, jnp.logical_not(first)):
+                scores = lax.dot_general(
+                    key, jnp.where(own, query, jnp.zeros_like(query)),
+                    (((1,), (1,)), ((), ())), preferred_element_type=F32)
+                weights = jnp.exp(scores - jnp.max(scores, axis=0, keepdims=True))
+                weights = (weights * (1.0 / jnp.sum(weights, axis=0, keepdims=True))).astype(BF16)
+                mixed.append(lax.dot_general(
+                    weights, value, (((0,), (0,)), ((), ())), preferred_element_type=F32))
+            mixed_ref[:, cut] = jnp.where(first, mixed[0], mixed[1]).astype(BF16)
+        copies[5].wait()
         residual = x_ref[...].astype(F32) + jnp.dot(mixed_ref[...], o_buf[...], preferred_element_type=F32)
-        out_ref[...] = root_scale(residual, fgain_ref[...]).astype(BF16)
-
-
-def encode(slot, counts, context, taken, weights):
-    square = pltpu.VMEM((D_ENC, D_ENC), BF16)
+        final_ref[...] = root_scale(residual, fgain_ref[...]).astype(BF16)
+        copy = pltpu.make_async_copy(final_ref, out_ref, sems.at[6])
+        copy.start()
+        copy.wait()
+
+
+def encode(slot, counts, context, taken, weights, *rows):
+    square, block = pltpu.VMEM((D_ENC, D_ENC), BF16), pltpu.VMEM((BLOCK, D_ENC), BF16)
+    piece = rows[0].shape if slot else (HALF_HEADS, LINES, LANES)
+    rows_out = (
+        [jax.ShapeDtypeStruct((2,) + piece, BF16)] if slot else [jax.ShapeDtypeStruct(piece, BF16)] * 2)
     return pl.pallas_call(
         functools.partial(encoder_kernel, slot),
-        out_shape=jax.ShapeDtypeStruct((BLOCK, D_ENC), BF16),
-        in_specs=[SMEM] + [HBM] * 6 + [VMEM] * 4,
-        out_specs=VMEM,
-        scratch_shapes=[
-            pltpu.VMEM((BLOCK, D_ENC), BF16), pltpu.VMEM((BLOCK, D_ENC), BF16),
-            square, square, square, square,
-            pltpu.SemaphoreType.DMA((PARTS, 4)), pltpu.SemaphoreType.DMA,
-        ],
+        out_shape=[jax.ShapeDtypeStruct((BLOCK, D_ENC), BF16)] + rows_out,
+        in_specs=[SMEM] + [HBM] * 7 + [VMEM] * (2 + len(rows)),
+        out_specs=[HBM] + [VMEM] * len(rows_out),
+        scratch_shapes=[block] * 6 + [pltpu.VMEM((2, BLOCK, LANES), F32)] + [square] * 4
+        + [pltpu.SemaphoreType.DMA((7,))],
         compiler_params=pltpu.CompilerParams(vmem_limit_bytes=63 * 2**20),
         cost_estimate=pl.CostEstimate(flops=6 * 10**9, bytes_accessed=9 * 2**20, transcendentals=2**20),
-    )(counts, context, taken, *weights)
+    )(counts, context, taken, *weights, *rows)
 
 
 def three_parts(values):
@@ -191,7 +191,8 @@
 
 def cross_kernel(counts_ref, *refs):
     tokens, loads, rows = refs[:6], refs[6:14], refs[14:18]
-    out_ref, token_buf, weight_buf, query_buf, total_ref, top_ref, sum_ref, sems, token_sems, row_sems = refs[18:]
+    out_ref, token_buf, weight_buf, query_buf, score_ref, value_ref, total_ref, top_ref, sum_ref = refs[18:27]
+    sems, token_sems, row_sems = refs[27:]
     me = lax.axis_index("ctx")
     core = lax.rem(me, 2)
     own_live, other_live, _ = live_counts(counts_ref)
@@ -233,36 +234,37 @@
         def _():
             token_copy(at).wait()
             both = jnp.dot(token_buf[at], weight_buf[...], preferred_element_type=F32).astype(BF16)
+            value_ref[at] = both[:, HALF_HEADS * LANES :]
             for head in range(HALF_HEADS):
-                key = both[:, head * LANES : (head + 1) * LANES]
-                value = both[:, (HALF_HEADS + head) * LANES : (HALF_HEADS + head + 1) * LANES]
                 scores = lax.dot_general(
-                    query_buf[head], key, (((1,), (1,)), ((), ())), preferred_element_type=F32
+                    both[:, head * LANES : (head + 1) * LANES], query_buf[head],
+                    (((1,), (1,)), ((), ())), preferred_element_type=F32,
                 ) * (1.0 / math.sqrt(HEAD_DIM))
-                old_top = top_ref[head]
-                new_top = jnp.maximum(old_top, jnp.max(scores, axis=-1, keepdims=True))
-                weights = jnp.exp(scores - new_top[:, :1])
-                shrink = jnp.exp(old_top - new_top)
-                top_ref[head] = new_top
-                sum_ref[head] = sum_ref[head] * shrink + jnp.sum(weights, axis=-1, keepdims=True)
-                total_ref[head] = total_ref[head] * shrink + jnp.dot(
-                    weights.astype(BF16), value, preferred_element_type=F32)
+                score_ref[at, head] = scores
+                top_ref[head] = jnp.maximum(top_ref[head], jnp.max(scores, axis=0, keepdims=True))
+
+    for at in range(2 * CAP):
+        @pl.when(live(at))
+        def _():
+            for head in range(HALF_HEADS):
+                weights = jnp.exp(score_ref[at, head] - top_ref[head])
+                sum_ref[head] += jnp.sum(weights, axis=0, keepdims=True)
+                total_ref[head] += lax.dot_general(
+                    weights.astype(BF16), value_ref[at, :, head * LANES : (head + 1) * LANES],
+                    (((0,), (0,)), ((), ())), preferred_element_type=F32)
 
     lines = total_ref.shape[1]
-    places = out_ref.shape[0] * 2
-    lane = lax.broadcasted_iota(jnp.int32, (lines, LANES), 1)
-    notes = jnp.zeros((lines, LANES), F32)
+    notes = []
     for head in range(HALF_HEADS):
-        pieces = three_parts(top_ref[head]) + three_parts(sum_ref[head])
-        for at, piece in enumerate(pieces):
-            notes = jnp.where(lane == 6 * head + at, piece, notes)
-        out_ref[:, :, head] = total_ref[head].astype(BF16).reshape(places // 2, 2, LINES, LANES)
-    out_ref[:, :, HALF_HEADS] = notes.astype(BF16).reshape(places // 2, 2, LINES, LANES)
+        notes += list(three_parts(top_ref[head])) + list(three_parts(sum_ref[head]))
+        out_ref[:, :, head] = total_ref[head].astype(BF16).reshape(CHIPS, 2, LINES, LANES)
+    notes = jnp.concatenate(notes + [jnp.zeros((LANES - len(notes), lines), F32)], axis=0).T
+    out_ref[:, :, HALF_HEADS] = notes.astype(BF16).reshape(CHIPS, 2, LINES, LANES)
 
 
 def cross(counts, tokens, loads, rows):
     lines = 2 * CHIPS * LINES
-    sums = pltpu.VMEM((HALF_HEADS, lines, LANES), F32)
+    line = pltpu.VMEM((HALF_HEADS, 1, lines), F32)
     return pl.pallas_call(
         cross_kernel,
         out_shape=jax.ShapeDtypeStruct((CHIPS, 2, HALF_HEADS + 1, LINES, LANES), BF16),
@@ -272,7 +274,10 @@
             pltpu.VMEM((2 * CAP, BLOCK, D_ENC), BF16),
             pltpu.VMEM((D_ENC, KV_HEADS * LANES), BF16),
             pltpu.VMEM((HALF_HEADS, lines, LANES), BF16),
-            sums, sums, sums,
+            pltpu.VMEM((2 * CAP, HALF_HEADS, BLOCK, lines), F32),
+            pltpu.VMEM((2 * CAP, BLOCK, HALF_HEADS * LANES), BF16),
+            pltpu.VMEM((HALF_HEADS, lines, LANES), F32),
+            line, line,
             pltpu.SemaphoreType.DMA((8,)), pltpu.SemaphoreType.DMA((2 * CAP,)), pltpu.SemaphoreType.DMA((16,)),
         ],
         compiler_params=pltpu.CompilerParams(vmem_limit_bytes=63 * 2**20),
@@ -329,8 +334,14 @@
     return lax.ppermute(values, "ctx", [(i, i ^ bits) for i in range(2 * CHIPS)])
 
 
-def round_z(values):
-    return lax.ppermute(values, "ctx", [(i, 4 * NEXT_Z[i // 4] + i % 4) for i in range(2 * CHIPS)])
+def round_z(values, steps=1):
+    ring = []
+    for i in range(2 * CHIPS):
+        z = i // 4
+        for _ in range(steps):
+            z = NEXT_Z[z]
+        ring.append((i, 4 * z + i % 4))
+    return lax.ppermute(values, "ctx", ring)
 
 
 def after(values, *others):
@@ -342,36 +353,29 @@
     load0 = w_kv
     load1 = round_z(load0)
     beside0 = exchange(load0, 2)
-    taken = exchange(context[2], 1)
-    keep, give = split_queries(queries)
-    row_chip = jnp.stack([keep, exchange(give, 1)])
-
-    cosine, sine = rotary_lanes()
-    weights = (w_query, w_key, w_value, w_out, norm_gain[None], final_gain[None], cosine, sine)
-    token0 = encode(0, counts, context, context, weights)
-    load1, row_chip, token0, taken = lax.optimization_barrier((load1, row_chip, token0, taken))
+    taken = exchange(context, 1)
+    weights = (w_query, w_key, w_value, w_out, rotary_lanes(), norm_gain, final_gain)
+    token0, keep, give = encode(0, counts, context, context, weights, queries)
+    load1, token0, keep, give, taken = lax.optimization_barrier((load1, token0, keep, give, taken))
     load2 = round_z(load1)
     beside1 = exchange(load1, 2)
+    got = exchange(give, 1)
     far0 = exchange(token0, 1)
+    token1, row_chip = encode(1, after(counts, beside0), context, taken, weights, keep, got)
+    load2, token1, row_chip = lax.optimization_barrier((load2, token1, row_chip))
+    load3 = round_z(load2)
     row_beside = exchange(row_chip, 2)
-    token1 = encode(1, after(counts, beside0), context, taken, weights)
-    load2, token1, row_beside = lax.optimization_barrier((load2, token1, row_beside))
-    load3 = round_z(load2)
     beside2 = exchange(load2, 2)
     far1 = exchange(token1, 1)
-    rows0 = jnp.stack([row_chip, row_beside])
-    rows1 = round_z(rows0)
-    token2 = encode(2, after(counts, beside1, far0), context, context, weights)
-    load3, token2, rows1 = lax.optimization_barrier((load3, token2, rows1))
+    token2, rows0 = encode(2, after(counts, beside1, far0), context, context, weights, row_chip, row_beside)
+    load3, token2, rows0 = lax.optimization_barrier((load3, token2, rows0))
     beside3 = exchange(load3, 2)
+    rows = [rows0] + [round_z(rows0, steps) for steps in (1, 2, 3)]
     far2 = exchange(token2, 1)
-    rows2 = round_z(rows1)
-    rows3 = round_z(rows2)
 
     parts = cross(
         counts, (token0, token1, token2, far0, far1, far2),
-        (load0, beside0, load1, beside1, load2, beside2, load3, beside3),
-        (rows0, rows1, rows2, rows3),
+        (load0, beside0, load1, beside1, load2, beside2, load3, beside3), rows,
     )
     arrived = [
         exchange(lax.dynamic_index_in_dim(parts, (me // 2) ^ chip, keepdims=False), 2 * chip)

time: 103 us -> 85.8 us (0.83)
  Pallas kernels: 47.1 us -> 31.6 us
  waiting for transfers between devices: 24.3 us -> 19.2 us
  starting transfers between devices: 23.8 us -> 28.8 us
  local copies, waits for them, and re-layouts: 7.33 us -> 4.92 us
    ppermute x6, waiting for transfers between devices: 16.3 us -> 5.68 us  [round_z(): return lax.ppermute(values, 'ctx', ring)]
    pallas_call x4 -> x3, Pallas kernels: 29 us -> 20.3 us  [encode(): pl.pallas_call(functools.partial(encoder_kernel, slot), out_shape=[jax.Sh...]
    ppermute x6, starting transfers between devices: 5.78 us -> 12.8 us  [round_z(): return lax.ppermute(values, 'ctx', ring)]
    pallas_call x1, Pallas kernels: 14.6 us -> 7.79 us  [cross(): pl.pallas_call(cross_kernel, out_shape=jax.ShapeDtypeStruct((CHIPS, 2, HA...]
    ppermute x18, waiting for transfers between devices: 8.09 us -> 13.5 us  [exchange(): lax.ppermute(values, 'ctx', [(i, i ^ bits) for i in range(2 * CHIPS)])]
    broadcast_in_dim x2 -> x0, local copies, waits for them, and re-layouts: 2.54 us -> none  [the longest x1 1.27 us: local(): final_gain[None]]
    ppermute x18, starting transfers between devices: 18.1 us -> 15.9 us  [exchange(): lax.ppermute(values, 'ctx', [(i, i ^ bits) for i in range(2 * CHIPS)])]
    unnamed x36 -> x38, local copies, waits for them, and re-layouts: 2.78 us -> 3.98 us
  transfers between devices with their start and end apart: 24 -> 24, of which waited for: 9 -> 9; matrix products, arithmetic and copies ran while one was open for 4% -> 0% of each run, Pallas kernels for 28% -> 24%
where the time goes in v1:
time: 85.8 us; the launch traced here: 84.8 us
  Pallas kernels  31.6 us (37%)
  starting transfers between devices  28.8 us (34%)
  waiting for transfers between devices  19.2 us (22%)
  local copies, waits for them, and re-layouts  4.92 us (6%)
    pallas_call x3, Pallas kernels, encode(): pl.pallas_call(functools.partial(encoder_kernel, slot), out_shape=[jax.Sh...  20.3 us
    ppermute x18, starting transfers between devices, exchange(): lax.ppermute(values, 'ctx', [(i, i ^ bits) for i in range(2 * CHIPS)])  15.9 us
    ppermute x18, waiting for transfers between devices, exchange(): lax.ppermute(values, 'ctx', [(i, i ^ bits) for i in range(2 * CHIPS)])  13.5 us
    ppermute x6, starting transfers between devices, round_z(): return lax.ppermute(values, 'ctx', ring)  12.8 us
    pallas_call x1, Pallas kernels, cross(): pl.pallas_call(cross_kernel, out_shape=jax.ShapeDtypeStruct((CHIPS, 2, HA...  7.79 us
    ppermute x6, waiting for transfers between devices, round_z(): return lax.ppermute(values, 'ctx', ring)  5.68 us
    unnamed x38, local copies, waits for them, and re-layouts  3.98 us
    pallas_call x1, Pallas kernels, combine(): pl.pallas_call(combine_kernel, out_shape=(shape, shape), in_specs=[VMEM]...  2.17 us
  transfers between devices with their start and end apart: 24, of which 9 were waited for; matrix products, arithmetic and copies ran while one was open for 0% of the time, Pallas kernels for 24%

profile of v1, /device:TPU:0, one launch (start us, length us, event | category | flops | bytes accessed | tf_op | source)
XLA Modules:
  0.0 84.8 jit_solution(4656442493407301241)
XLA Ops:
  0.5 2.6 %collective-permute-start = (bf16[1024,128]{1,0:T(8,128)(2,1)}, bf16[1024,128]{1,0:T(8,128)(2,1)S(1)}, u32[]{:S(2)}, u32[]{:S(2)}) collective-permute-start(bf16[1024,128]{1,0:T(8,128)(2,1)} %refs_6_.1), channel_id=1, source_target_pairs={{0,4},{1,5},{2,6},{3,7},{4,12},{5,13},{6,14},{7,15},{8,0},{9,1},{1... | collective-permute-start | bytes 786440 | tf_op jit(solution)/shard_map/ppermute | solution.py:344
  3.0 1.5 %collective-permute-start.3 = (bf16[1024,128]{1,0:T(8,128)(2,1)}, bf16[1024,128]{1,0:T(8,128)(2,1)S(1)}, u32[]{:S(2)}, u32[]{:S(2)}) collective-permute-start(bf16[1024,128]{1,0:T(8,128)(2,1)} %refs_6_.1), channel_id=1, source_target_pairs={{0,2},{1,3},{2,0},{3,1},{4,6},{5,7},{6,4},{7,5},{8,10},{9,11},{10,... | collective-permute-start | bytes 786440 | tf_op jit(solution)/shard_map/ppermute | solution.py:334
  4.5 9.3 %shard_map.109 = (bf16[256,1024]{1,0:T(8,128)(2,1)}, bf16[4,16,128]{2,1,0:T(8,128)(2,1)}, bf16[4,16,128]{2,1,0:T(8,128)(2,1)}) custom-call(s32[16]{0:T(128)} %counts_ref.5, bf16[3,256,1024]{2,1,0:T(8,128)(2,1)} %taken_ref.3, bf16[3,256,1024]{2,1,0:T(8,128)(2,1)} %taken_ref.3, bf16[1024,1024]{1,0:T(8,128)(2,1)} %wq_ref.5, bf16[1024,1024]{1,0:T(8,128)(2,1)} %wk_ref.5, ...), custom_call_target="tpu_custom_call" | custom-call | flops 6000000000 | bytes 9437184 | tf_op jit(solution)/shard_map/pallas_call | solution.py:163
  14.0 2.6 %collective-permute-start.2 = (bf16[1024,128]{1,0:T(8,128)(2,1)S(1)}, bf16[1024,128]{1,0:T(8,128)(2,1)}, u32[]{:S(2)}, u32[]{:S(2)}) collective-permute-start(bf16[1024,128]{1,0:T(8,128)(2,1)S(1)} %collective-permute-done.refs_8_), channel_id=1, source_target_pairs={{0,4},{1,5},{2,6},{3,7},{4,12},{5,13},{6,14},{7,15},{8,0},{9,1},{1... | collective-permute-start | bytes 786440 | tf_op jit(solution)/shard_map/ppermute | solution.py:344
  17.7 9.3 %shard_map.110 = (bf16[256,1024]{1,0:T(8,128)(2,1)}, bf16[2,4,16,128]{3,2,1,0:T(8,128)(2,1)}) custom-call(s32[16]{0:T(128)} %counts_ref.5, bf16[3,256,1024]{2,1,0:T(8,128)(2,1)} %taken_ref.3, bf16[3,256,1024]{2,1,0:T(8,128)(2,1)} %collective-permute-done.1.taken_ref, bf16[1024,1024]{1,0:T(8,128)(2,1)} %wq_ref.5, bf16[1024,1024]{1,0:T(8,128)(2,1)} %wk_ref.5, ...), custom_call_target="tpu_custom_call" | custom-call | flops 6000000000 | bytes 9437184 | tf_op jit(solution)/shard_map/pallas_call | solution.py:163
  27.1 2.3 %collective-permute-start.5 = (bf16[1024,128]{1,0:T(8,128)(2,1)}, bf16[1024,128]{1,0:T(8,128)(2,1)}, u32[]{:S(2)}, u32[]{:S(2)}) collective-permute-start(bf16[1024,128]{1,0:T(8,128)(2,1)} %collective-permute-done.2.refs_10_), channel_id=1, source_target_pairs={{0,4},{1,5},{2,6},{3,7},{4,12},{5,13},{6,14},{7,15},{8,0},{9,1},{1... | collective-permute-start | bytes 786440 | tf_op jit(solution)/shard_map/ppermute | solution.py:344
  29.5 1.7 %collective-permute-done.8.refs_1_ = bf16[2,4,16,128]{3,2,1,0:T(8,128)(2,1)S(1)} collective-permute-done((bf16[2,4,16,128]{3,2,1,0:T(8,128)(2,1)}, bf16[2,4,16,128]{3,2,1,0:T(8,128)(2,1)S(1)}, u32[]{:S(2)}, u32[]{:S(2)}) %collective-permute-start.8) | collective-permute-done | bytes 32800 | tf_op jit(solution)/shard_map/ppermute | solution.py:334
  31.9 1.7 %shard_map.111 = (bf16[256,1024]{1,0:T(8,128)(2,1)}, bf16[2,2,4,16,128]{4,3,2,1,0:T(8,128)(2,1)}) custom-call(s32[16]{0:T(128)} %counts_ref.5, bf16[3,256,1024]{2,1,0:T(8,128)(2,1)} %taken_ref.3, bf16[3,256,1024]{2,1,0:T(8,128)(2,1)} %taken_ref.3, bf16[1024,1024]{1,0:T(8,128)(2,1)} %wq_ref.5, bf16[1024,1024]{1,0:T(8,128)(2,1)} %wk_ref.5, ...), custom_call_target="tpu_custom_call" | custom-call | flops 6000000000 | bytes 9437184 | tf_op jit(solution)/shard_map/pallas_call | solution.py:163
  33.6 1.3 %collective-permute-done.5.refs_12_ = bf16[1024,128]{1,0:T(8,128)(2,1)} collective-permute-done((bf16[1024,128]{1,0:T(8,128)(2,1)}, bf16[1024,128]{1,0:T(8,128)(2,1)}, u32[]{:S(2)}, u32[]{:S(2)}) %collective-permute-start.5) | collective-permute-done | bytes 262176 | tf_op jit(solution)/shard_map/ppermute | solution.py:344
  34.8 1.9 %collective-permute-start.11 = (bf16[1024,128]{1,0:T(8,128)(2,1)}, bf16[1024,128]{1,0:T(8,128)(2,1)S(1)}, u32[]{:S(2)}, u32[]{:S(2)}) collective-permute-start(bf16[1024,128]{1,0:T(8,128)(2,1)} %collective-permute-done.2.refs_10_), channel_id=1, source_target_pairs={{0,2},{1,3},{2,0},{3,1},{4,6},{5,7},{6,4},{7,5},{8,10},{9,11},{10,... | collective-permute-start | bytes 786440 | tf_op jit(solution)/shard_map/ppermute | solution.py:334
  36.9 1.4 %collective-permute-start.13 = (bf16[2,2,4,16,128]{4,3,2,1,0:T(8,128)(2,1)}, bf16[2,2,4,16,128]{4,3,2,1,0:T(8,128)(2,1)S(1)}, u32[]{:S(2)}, u32[]{:S(2)}) collective-permute-start(bf16[2,2,4,16,128]{4,3,2,1,0:T(8,128)(2,1)} %get-tuple-element.46.refs_14_), channel_id=1, source_target_pairs={{0,4},{1,5},{2,6},{3,7},{4,12},{5,13},{6,14},{7,15},{8,0},{9,1},{1... | collective-permute-start | bytes 196616 | tf_op jit(solution)/shard_map/ppermute | solution.py:344
  38.2 6.0 %collective-permute-done.11.refs_11_ = bf16[1024,128]{1,0:T(8,128)(2,1)S(1)} collective-permute-done((bf16[1024,128]{1,0:T(8,128)(2,1)}, bf16[1024,128]{1,0:T(8,128)(2,1)S(1)}, u32[]{:S(2)}, u32[]{:S(2)}) %collective-permute-start.11) | collective-permute-done | bytes 262176 | tf_op jit(solution)/shard_map/ppermute | solution.py:334
  44.2 3.9 %collective-permute-start.14 = (bf16[2,2,4,16,128]{4,3,2,1,0:T(8,128)(2,1)}, bf16[2,2,4,16,128]{4,3,2,1,0:T(8,128)(2,1)S(1)}, u32[]{:S(2)}, u32[]{:S(2)}) collective-permute-start(bf16[2,2,4,16,128]{4,3,2,1,0:T(8,128)(2,1)} %get-tuple-element.46.refs_14_), channel_id=1, source_target_pairs={{0,12},{1,13},{2,14},{3,15},{4,8},{5,9},{6,10},{7,11},{8,4},{9,5},... | collective-permute-start | bytes 196616 | tf_op jit(solution)/shard_map/ppermute | solution.py:344
  48.2 2.7 %collective-permute-done.14.refs_16_ = bf16[2,2,4,16,128]{4,3,2,1,0:T(8,128)(2,1)S(1)} collective-permute-done((bf16[2,2,4,16,128]{4,3,2,1,0:T(8,128)(2,1)}, bf16[2,2,4,16,128]{4,3,2,1,0:T(8,128)(2,1)S(1)}, u32[]{:S(2)}, u32[]{:S(2)}) %collective-permute-start.14) | collective-permute-done | bytes 65568 | tf_op jit(solution)/shard_map/ppermute | solution.py:344
  50.9 1.8 %collective-permute-done.15.refs_17_ = bf16[2,2,4,16,128]{4,3,2,1,0:T(8,128)(2,1)S(1)} collective-permute-done((bf16[2,2,4,16,128]{4,3,2,1,0:T(8,128)(2,1)}, bf16[2,2,4,16,128]{4,3,2,1,0:T(8,128)(2,1)S(1)}, u32[]{:S(2)}, u32[]{:S(2)}) %collective-permute-start.15) | collective-permute-done | bytes 65568 | tf_op jit(solution)/shard_map/ppermute | solution.py:344
  54.2 7.8 %shard_map.112.refs_0_ = bf16[8,2,5,16,128]{4,3,2,1,0:T(8,128)(2,1)} custom-call(s32[16]{0:T(128)} %counts_ref.5, bf16[256,1024]{1,0:T(8,128)(2,1)} %get-tuple-element.30.refs_0_, bf16[256,1024]{1,0:T(8,128)(2,1)} %get-tuple-element.38.refs_1_, bf16[256,1024]{1,0:T(8,128)(2,1)} %get-tuple-element.44.refs_2_, bf16[256,1024]{1,0:T(8,128)(2,1)} %copy-done.8, ...), custom_call_target="tpu_custom_call" | custom-call | flops 6000000000 | bytes 8388608 | tf_op jit(solution)/shard_map/pallas_call | solution.py:268
  64.0 2.5 %collective-permute-start.18 = (bf16[2,5,16,128]{3,2,1,0:T(8,128)(2,1)S(1)}, bf16[2,5,16,128]{3,2,1,0:T(8,128)(2,1)S(1)}, u32[]{:S(2)}, u32[]{:S(2)}) collective-permute-start(bf16[2,5,16,128]{3,2,1,0:T(8,128)(2,1)S(1)} %get-tuple-element.53), channel_id=1, source_target_pairs={{0,6},{1,7},{2,4},{3,5},{4,2},{5,3},{6,0},{7,1},{8,14},{9,15},{10,... | collective-permute-start | bytes 122888 | tf_op jit(solution)/shard_map/ppermute | solution.py:334
  66.5 3.0 %collective-permute-start.19 = (bf16[2,5,16,128]{3,2,1,0:T(8,128)(2,1)S(1)}, bf16[2,5,16,128]{3,2,1,0:T(8,128)(2,1)S(1)}, u32[]{:S(2)}, u32[]{:S(2)}) collective-permute-start(bf16[2,5,16,128]{3,2,1,0:T(8,128)(2,1)S(1)} %get-tuple-element.52), channel_id=1, source_target_pairs={{0,8},{1,9},{2,10},{3,11},{4,12},{5,13},{6,14},{7,15},{8,0},{9,1},... | collective-permute-start | bytes 122888 | tf_op jit(solution)/shard_map/ppermute | solution.py:334
  69.5 2.4 %collective-permute-start.21 = (bf16[2,5,16,128]{3,2,1,0:T(8,128)(2,1)S(1)}, bf16[2,5,16,128]{3,2,1,0:T(8,128)(2,1)S(1)}, u32[]{:S(2)}, u32[]{:S(2)}) collective-permute-start(bf16[2,5,16,128]{3,2,1,0:T(8,128)(2,1)S(1)} %get-tuple-element.50), channel_id=1, source_target_pairs={{0,12},{1,13},{2,14},{3,15},{4,8},{5,9},{6,10},{7,11},{8,4},{9,5},... | collective-permute-start | bytes 122888 | tf_op jit(solution)/shard_map/ppermute | solution.py:334
  71.9 2.4 %collective-permute-start.22 = (bf16[2,5,16,128]{3,2,1,0:T(8,128)(2,1)S(1)}, bf16[2,5,16,128]{3,2,1,0:T(8,128)(2,1)S(1)}, u32[]{:S(2)}, u32[]{:S(2)}) collective-permute-start(bf16[2,5,16,128]{3,2,1,0:T(8,128)(2,1)S(1)} %get-tuple-element.49), channel_id=1, source_target_pairs={{0,14},{1,15},{2,12},{3,13},{4,10},{5,11},{6,8},{7,9},{8,6},{9,7},... | collective-permute-start | bytes 122888 | tf_op jit(solution)/shard_map/ppermute | solution.py:334
  75.5 3.1 %collective-permute-done.22.refs_7_ = bf16[2,5,16,128]{3,2,1,0:T(8,128)(2,1)S(1)} collective-permute-done((bf16[2,5,16,128]{3,2,1,0:T(8,128)(2,1)S(1)}, bf16[2,5,16,128]{3,2,1,0:T(8,128)(2,1)S(1)}, u32[]{:S(2)}, u32[]{:S(2)}) %collective-permute-start.22) | collective-permute-done | bytes 40992 | tf_op jit(solution)/shard_map/ppermute | solution.py:334
  79.2 2.2 %shard_map.113 = (bf16[4,16,128]{2,1,0:T(8,128)(2,1)}, bf16[4,16,128]{2,1,0:T(8,128)(2,1)}) custom-call(bf16[8,2,5,16,128]{4,3,2,1,0:T(8,128)(2,1)} %shard_map.112.refs_0_, bf16[2,5,16,128]{3,2,1,0:T(8,128)(2,1)} %copy-done, bf16[2,5,16,128]{3,2,1,0:T(8,128)(2,1)} %copy-done.1, bf16[2,5,16,128]{3,2,1,0:T(8,128)(2,1)} %copy-done.2, ...), custom_call_target="tpu_custom_call" | custom-call | tf_op jit(solution)/shard_map/pallas_call | solution.py:309
  81.4 1.4 %collective-permute-done.23.got_ref = bf16[4,16,128]{2,1,0:T(8,128)(2,1)S(1)} collective-permute-done((bf16[4,16,128]{2,1,0:T(8,128)(2,1)}, bf16[4,16,128]{2,1,0:T(8,128)(2,1)S(1)}, u32[]{:S(2)}, u32[]{:S(2)}) %collective-permute-start.23) | collective-permute-done | bytes 16416 | tf_op jit(solution)/shard_map/ppermute | solution.py:334
  83.4 1.4 %shard_map.114 = bf16[4,4096]{1,0:T(4,128)(2,1)} custom-call(bf16[4,16,128]{2,1,0:T(8,128)(2,1)} %get-tuple-element.47.keep_ref, bf16[4,16,128]{2,1,0:T(8,128)(2,1)} %copy-done.7), custom_call_target="tpu_custom_call" | custom-call | tf_op jit(solution)/shard_map/pallas_call | solution.py:325
  (69 shorter events, 8.4 us)
Async XLA Ops:
  0.0 13.9 %collective-permute-start.1 = (bf16[3,256,1024]{2,1,0:T(8,128)(2,1)}, bf16[3,256,1024]{2,1,0:T(8,128)(2,1)}, u32[]{:S(2)}, u32[]{:S(2)}) collective-permute-start(bf16[3,256,1024]{2,1,0:T(8,128)(2,1)} %taken_ref.3), channel_id=1, source_target_pairs={{0,1},{1,0},{2,3},{3,2},{4,5},{5,4},{6,7},{7,6},{8,9},{9,8},{10,11... | collective-permute-start | bytes 4718600 | tf_op jit(solution)/shard_map/ppermute | solution.py:334
  0.5 13.4 %collective-permute-start = (bf16[1024,128]{1,0:T(8,128)(2,1)}, bf16[1024,128]{1,0:T(8,128)(2,1)S(1)}, u32[]{:S(2)}, u32[]{:S(2)}) collective-permute-start(bf16[1024,128]{1,0:T(8,128)(2,1)} %refs_6_.1), channel_id=1, source_target_pairs={{0,4},{1,5},{2,6},{3,7},{4,12},{5,13},{6,14},{7,15},{8,0},{9,1},{1... | collective-permute-start | bytes 786440 | tf_op jit(solution)/shard_map/ppermute | solution.py:344
  3.0 10.9 %collective-permute-start.3 = (bf16[1024,128]{1,0:T(8,128)(2,1)}, bf16[1024,128]{1,0:T(8,128)(2,1)S(1)}, u32[]{:S(2)}, u32[]{:S(2)}) collective-permute-start(bf16[1024,128]{1,0:T(8,128)(2,1)} %refs_6_.1), channel_id=1, source_target_pairs={{0,2},{1,3},{2,0},{3,1},{4,6},{5,7},{6,4},{7,5},{8,10},{9,11},{10,... | collective-permute-start | bytes 786440 | tf_op jit(solution)/shard_map/ppermute | solution.py:334
  13.9 3.3 %collective-permute-start.4 = (bf16[4,16,128]{2,1,0:T(8,128)(2,1)}, bf16[4,16,128]{2,1,0:T(8,128)(2,1)S(1)}, u32[]{:S(2)}, u32[]{:S(2)}) collective-permute-start(bf16[4,16,128]{2,1,0:T(8,128)(2,1)} %get-tuple-element.35), channel_id=1, source_target_pairs={{0,1},{1,0},{2,3},{3,2},{4,5},{5,4},{6,7},{7,6},{8,9},{9,8},{10,11... | collective-permute-start | bytes 49160 | tf_op jit(solution)/shard_map/ppermute | solution.py:334
  14.0 13.1 %collective-permute-start.2 = (bf16[1024,128]{1,0:T(8,128)(2,1)S(1)}, bf16[1024,128]{1,0:T(8,128)(2,1)}, u32[]{:S(2)}, u32[]{:S(2)}) collective-permute-start(bf16[1024,128]{1,0:T(8,128)(2,1)S(1)} %collective-permute-done.refs_8_), channel_id=1, source_target_pairs={{0,4},{1,5},{2,6},{3,7},{4,12},{5,13},{6,14},{7,15},{8,0},{9,1},{1... | collective-permute-start | bytes 786440 | tf_op jit(solution)/shard_map/ppermute | solution.py:344
  16.6 12.9 %collective-permute-start.6 = (bf16[1024,128]{1,0:T(8,128)(2,1)S(1)}, bf16[1024,128]{1,0:T(8,128)(2,1)}, u32[]{:S(2)}, u32[]{:S(2)}) collective-permute-start(bf16[1024,128]{1,0:T(8,128)(2,1)S(1)} %collective-permute-done.refs_8_), channel_id=1, source_target_pairs={{0,2},{1,3},{2,0},{3,1},{4,6},{5,7},{6,4},{7,5},{8,10},{9,11},{10,... | collective-permute-start | bytes 786440 | tf_op jit(solution)/shard_map/ppermute | solution.py:334
  17.1 12.4 %collective-permute-start.7 = (bf16[256,1024]{1,0:T(8,128)(2,1)}, bf16[256,1024]{1,0:T(8,128)(2,1)S(1)}, u32[]{:S(2)}, u32[]{:S(2)}) collective-permute-start(bf16[256,1024]{1,0:T(8,128)(2,1)} %get-tuple-element.30.refs_0_), channel_id=1, source_target_pairs={{0,1},{1,0},{2,3},{3,2},{4,5},{5,4},{6,7},{7,6},{8,9},{9,8},{10,11... | collective-permute-start | bytes 1572872 | tf_op jit(solution)/shard_map/ppermute | solution.py:334
  27.1 4.2 %collective-permute-start.8 = (bf16[2,4,16,128]{3,2,1,0:T(8,128)(2,1)}, bf16[2,4,16,128]{3,2,1,0:T(8,128)(2,1)S(1)}, u32[]{:S(2)}, u32[]{:S(2)}) collective-permute-start(bf16[2,4,16,128]{3,2,1,0:T(8,128)(2,1)} %get-tuple-element.41.refs_0_), channel_id=1, source_target_pairs={{0,2},{1,3},{2,0},{3,1},{4,6},{5,7},{6,4},{7,5},{8,10},{9,11},{10,... | collective-permute-start | bytes 98312 | tf_op jit(solution)/shard_map/ppermute | solution.py:334
  27.1 7.7 %collective-permute-start.5 = (bf16[1024,128]{1,0:T(8,128)(2,1)}, bf16[1024,128]{1,0:T(8,128)(2,1)}, u32[]{:S(2)}, u32[]{:S(2)}) collective-permute-start(bf16[1024,128]{1,0:T(8,128)(2,1)} %collective-permute-done.2.refs_10_), channel_id=1, source_target_pairs={{0,4},{1,5},{2,6},{3,7},{4,12},{5,13},{6,14},{7,15},{8,0},{9,1},{1... | collective-permute-start | bytes 786440 | tf_op jit(solution)/shard_map/ppermute | solution.py:344
  29.5 23.9 %collective-permute-start.9 = (bf16[256,1024]{1,0:T(8,128)(2,1)}, bf16[256,1024]{1,0:T(8,128)(2,1)}, u32[]{:S(2)}, u32[]{:S(2)}) collective-permute-start(bf16[256,1024]{1,0:T(8,128)(2,1)} %get-tuple-element.38.refs_1_), channel_id=1, source_target_pairs={{0,1},{1,0},{2,3},{3,2},{4,5},{5,4},{6,7},{7,6},{8,9},{9,8},{10,11... | collective-permute-start | bytes 1572872 | tf_op jit(solution)/shard_map/ppermute | solution.py:334
  34.8 18.5 %collective-permute-start.10 = (bf16[256,1024]{1,0:T(8,128)(2,1)}, bf16[256,1024]{1,0:T(8,128)(2,1)S(1)}, u32[]{:S(2)}, u32[]{:S(2)}) collective-permute-start(bf16[256,1024]{1,0:T(8,128)(2,1)} %get-tuple-element.44.refs_2_), channel_id=1, source_target_pairs={{0,1},{1,0},{2,3},{3,2},{4,5},{5,4},{6,7},{7,6},{8,9},{9,8},{10,11... | collective-permute-start | bytes 1572872 | tf_op jit(solution)/shard_map/ppermute | solution.py:334
  34.8 9.4 %collective-permute-start.11 = (bf16[1024,128]{1,0:T(8,128)(2,1)}, bf16[1024,128]{1,0:T(8,128)(2,1)S(1)}, u32[]{:S(2)}, u32[]{:S(2)}) collective-permute-start(bf16[1024,128]{1,0:T(8,128)(2,1)} %collective-permute-done.2.refs_10_), channel_id=1, source_target_pairs={{0,2},{1,3},{2,0},{3,1},{4,6},{5,7},{6,4},{7,5},{8,10},{9,11},{10,... | collective-permute-start | bytes 786440 | tf_op jit(solution)/shard_map/ppermute | solution.py:334
  36.8 15.9 %collective-permute-start.12 = (bf16[1024,128]{1,0:T(8,128)(2,1)}, bf16[1024,128]{1,0:T(8,128)(2,1)S(1)}, u32[]{:S(2)}, u32[]{:S(2)}) collective-permute-start(bf16[1024,128]{1,0:T(8,128)(2,1)} %collective-permute-done.5.refs_12_), channel_id=1, source_target_pairs={{0,2},{1,3},{2,0},{3,1},{4,6},{5,7},{6,4},{7,5},{8,10},{9,11},{10,... | collective-permute-start | bytes 786440 | tf_op jit(solution)/shard_map/ppermute | solution.py:334
  36.9 11.3 %collective-permute-start.13 = (bf16[2,2,4,16,128]{4,3,2,1,0:T(8,128)(2,1)}, bf16[2,2,4,16,128]{4,3,2,1,0:T(8,128)(2,1)S(1)}, u32[]{:S(2)}, u32[]{:S(2)}) collective-permute-start(bf16[2,2,4,16,128]{4,3,2,1,0:T(8,128)(2,1)} %get-tuple-element.46.refs_14_), channel_id=1, source_target_pairs={{0,4},{1,5},{2,6},{3,7},{4,12},{5,13},{6,14},{7,15},{8,0},{9,1},{1... | collective-permute-start | bytes 196616 | tf_op jit(solution)/shard_map/ppermute | solution.py:344
  44.2 6.6 %collective-permute-start.14 = (bf16[2,2,4,16,128]{4,3,2,1,0:T(8,128)(2,1)}, bf16[2,2,4,16,128]{4,3,2,1,0:T(8,128)(2,1)S(1)}, u32[]{:S(2)}, u32[]{:S(2)}) collective-permute-start(bf16[2,2,4,16,128]{4,3,2,1,0:T(8,128)(2,1)} %get-tuple-element.46.refs_14_), channel_id=1, source_target_pairs={{0,12},{1,13},{2,14},{3,15},{4,8},{5,9},{6,10},{7,11},{8,4},{9,5},... | collective-permute-start | bytes 196616 | tf_op jit(solution)/shard_map/ppermute | solution.py:344
  48.1 4.5 %collective-permute-start.15 = (bf16[2,2,4,16,128]{4,3,2,1,0:T(8,128)(2,1)}, bf16[2,2,4,16,128]{4,3,2,1,0:T(8,128)(2,1)S(1)}, u32[]{:S(2)}, u32[]{:S(2)}) collective-permute-start(bf16[2,2,4,16,128]{4,3,2,1,0:T(8,128)(2,1)} %get-tuple-element.46.refs_14_), channel_id=1, source_target_pairs={{0,8},{1,9},{2,10},{3,11},{4,0},{5,1},{6,2},{7,3},{8,12},{9,13},{1... | collective-permute-start | bytes 196616 | tf_op jit(solution)/shard_map/ppermute | solution.py:344
  62.9 6.6 %collective-permute-start.16 = (bf16[2,5,16,128]{3,2,1,0:T(8,128)(2,1)S(1)}, bf16[2,5,16,128]{3,2,1,0:T(8,128)(2,1)S(1)}, u32[]{:S(2)}, u32[]{:S(2)}) collective-permute-start(bf16[2,5,16,128]{3,2,1,0:T(8,128)(2,1)S(1)} %get-tuple-element.55), channel_id=1, source_target_pairs={{0,2},{1,3},{2,0},{3,1},{4,6},{5,7},{6,4},{7,5},{8,10},{9,11},{10,... | collective-permute-start | bytes 122888 | tf_op jit(solution)/shard_map/ppermute | solution.py:334
  63.0 8.9 %collective-permute-start.17 = (bf16[2,5,16,128]{3,2,1,0:T(8,128)(2,1)S(1)}, bf16[2,5,16,128]{3,2,1,0:T(8,128)(2,1)S(1)}, u32[]{:S(2)}, u32[]{:S(2)}) collective-permute-start(bf16[2,5,16,128]{3,2,1,0:T(8,128)(2,1)S(1)} %get-tuple-element.54), channel_id=1, source_target_pairs={{0,4},{1,5},{2,6},{3,7},{4,0},{5,1},{6,2},{7,3},{8,12},{9,13},{10,... | collective-permute-start | bytes 122888 | tf_op jit(solution)/shard_map/ppermute | solution.py:334
  64.0 10.3 %collective-permute-start.18 = (bf16[2,5,16,128]{3,2,1,0:T(8,128)(2,1)S(1)}, bf16[2,5,16,128]{3,2,1,0:T(8,128)(2,1)S(1)}, u32[]{:S(2)}, u32[]{:S(2)}) collective-permute-start(bf16[2,5,16,128]{3,2,1,0:T(8,128)(2,1)S(1)} %get-tuple-element.53), channel_id=1, source_target_pairs={{0,6},{1,7},{2,4},{3,5},{4,2},{5,3},{6,0},{7,1},{8,14},{9,15},{10,... | collective-permute-start | bytes 122888 | tf_op jit(solution)/shard_map/ppermute | solution.py:334
  66.5 7.8 %collective-permute-start.19 = (bf16[2,5,16,128]{3,2,1,0:T(8,128)(2,1)S(1)}, bf16[2,5,16,128]{3,2,1,0:T(8,128)(2,1)S(1)}, u32[]{:S(2)}, u32[]{:S(2)}) collective-permute-start(bf16[2,5,16,128]{3,2,1,0:T(8,128)(2,1)S(1)} %get-tuple-element.52), channel_id=1, source_target_pairs={{0,8},{1,9},{2,10},{3,11},{4,12},{5,13},{6,14},{7,15},{8,0},{9,1},... | collective-permute-start | bytes 122888 | tf_op jit(solution)/shard_map/ppermute | solution.py:334
  69.5 5.8 %collective-permute-start.20 = (bf16[2,5,16,128]{3,2,1,0:T(8,128)(2,1)S(1)}, bf16[2,5,16,128]{3,2,1,0:T(8,128)(2,1)S(1)}, u32[]{:S(2)}, u32[]{:S(2)}) collective-permute-start(bf16[2,5,16,128]{3,2,1,0:T(8,128)(2,1)S(1)} %get-tuple-element.51), channel_id=1, source_target_pairs={{0,10},{1,11},{2,8},{3,9},{4,14},{5,15},{6,12},{7,13},{8,2},{9,3},... | collective-permute-start | bytes 122888 | tf_op jit(solution)/shard_map/ppermute | solution.py:334
  69.5 6.0 %collective-permute-start.21 = (bf16[2,5,16,128]{3,2,1,0:T(8,128)(2,1)S(1)}, bf16[2,5,16,128]{3,2,1,0:T(8,128)(2,1)S(1)}, u32[]{:S(2)}, u32[]{:S(2)}) collective-permute-start(bf16[2,5,16,128]{3,2,1,0:T(8,128)(2,1)S(1)} %get-tuple-element.50), channel_id=1, source_target_pairs={{0,12},{1,13},{2,14},{3,15},{4,8},{5,9},{6,10},{7,11},{8,4},{9,5},... | collective-permute-start | bytes 122888 | tf_op jit(solution)/shard_map/ppermute | solution.py:334
  71.9 6.7 %collective-permute-start.22 = (bf16[2,5,16,128]{3,2,1,0:T(8,128)(2,1)S(1)}, bf16[2,5,16,128]{3,2,1,0:T(8,128)(2,1)S(1)}, u32[]{:S(2)}, u32[]{:S(2)}) collective-permute-start(bf16[2,5,16,128]{3,2,1,0:T(8,128)(2,1)S(1)} %get-tuple-element.49), channel_id=1, source_target_pairs={{0,14},{1,15},{2,12},{3,13},{4,10},{5,11},{6,8},{7,9},{8,6},{9,7},... | collective-permute-start | bytes 122888 | tf_op jit(solution)/shard_map/ppermute | solution.py:334
  81.4 1.4 %collective-permute-start.23 = (bf16[4,16,128]{2,1,0:T(8,128)(2,1)}, bf16[4,16,128]{2,1,0:T(8,128)(2,1)S(1)}, u32[]{:S(2)}, u32[]{:S(2)}) collective-permute-start(bf16[4,16,128]{2,1,0:T(8,128)(2,1)} %get-tuple-element.48), channel_id=1, source_target_pairs={{0,1},{1,0},{2,3},{3,2},{4,5},{5,4},{6,7},{7,6},{8,9},{9,8},{10,11... | collective-permute-start | bytes 49160 | tf_op jit(solution)/shard_map/ppermute | solution.py:334
  (19 other events, 72.4 us)
